TPU v7x, 32 devices: a whole 2x2x4 slice. The times are simulated.
32 devices in a mesh: dp: 4 (over x, core), ctx: 2 (over y), tensor: 4 (over z).
Axes of the slice: x: 2, y: 2, z: 4, core: 2. Of those that a mesh axis runs over, the one named last changes fastest.
Arguments:
- layer_input: bfloat16 [4, 1536, 2560], P('dp', 'ctx'), may hold values from -6 to 6
- cotangent: bfloat16 [4, 1536, 2560], P('dp', 'ctx'), may hold values from -6 to 6
- span_order: int32 [4], replicated, may hold values from 0 to 3, each once
- query_down: bfloat16 [2560, 768], P(('dp', 'ctx')), may hold values from -0.125 to 0.125
- latent_down: bfloat16 [2560, 288], P(('dp', 'ctx')), may hold values from -0.125 to 0.125
- query_up: bfloat16 [768, 3840], P(('dp', 'ctx'), 'tensor'), may hold values from -0.21875 to 0.21875
- latent_up: bfloat16 [256, 5120], P(('dp', 'ctx'), 'tensor'), may hold values from -0.375 to 0.375
- output_weight: bfloat16 [2560, 2560], P('tensor', ('dp', 'ctx')), may hold values from -4 to 4
- gate_weight: bfloat16 [2560, 6400], P(('dp', 'ctx'), 'tensor'), may hold values from -0.125 to 0.125
- up_weight: bfloat16 [2560, 6400], P(('dp', 'ctx'), 'tensor'), may hold values from -0.125 to 0.125
- down_weight: bfloat16 [6400, 2560], P('tensor', ('dp', 'ctx')), may hold values from -0.625 to 0.625
- first_gain: float32 [2560], replicated, may hold values from 0.25 to 1.75
- query_gain: float32 [768], replicated, may hold values from 0.25 to 1.75
- latent_gain: float32 [256], replicated, may hold values from 0.25 to 1.75
- second_gain: float32 [2560], replicated, may hold values from 0.25 to 1.75
Outputs:
- block_out: bfloat16 [4, 1536, 2560], P('dp', 'ctx')
- input_grad: float32 [4, 1536, 2560], P('dp', 'ctx')
- query_down_grad: float32 [2560, 768], P(('dp', 'ctx'), 'tensor')
- latent_down_grad: float32 [2560, 288], P(('dp', 'ctx'), 'tensor')
- query_up_grad: float32 [768, 3840], P(('dp', 'ctx'), 'tensor')
- latent_up_grad: float32 [256, 5120], P(('dp', 'ctx'), 'tensor')
- output_grad: float32 [2560, 2560], P('tensor', ('dp', 'ctx'))
- gate_grad: float32 [2560, 6400], P(('dp', 'ctx'), 'tensor')
- up_grad: float32 [2560, 6400], P(('dp', 'ctx'), 'tensor')
- down_grad: float32 [6400, 2560], P('tensor', ('dp', 'ctx'))
- first_gain_grad: float32 [2560], P(('dp', 'ctx'))
- query_gain_grad: float32 [768], P(('dp', 'ctx'))
- latent_gain_grad: float32 [256], P(('dp', 'ctx'))
- second_gain_grad: float32 [2560], P(('dp', 'ctx'))
Inputs may be any that keep to these rules, and one draw needn't show every extreme that they name: A permutation: stored block b of every sequence (384 tokens; a device of ctx holds two neighbouring stored blocks) holds positions span_order[b] * 384 onward.
All inputs are finite; a program needn't handle non-finite values.
Results may differ from a plain program's by a relative error of at most 0.025.
Values may be sent and summed in bfloat16 or wider, within the bound.
No kernel may reach another device: no remote copies, remote signals or barrier semaphores. Data moves between devices by JAX's collectives and lax.ppermute only.
A program may use at most 256 MiB of HBM per device.

v0:
```python
import math

import jax
import jax.numpy as jnp
from jax import lax
from jax.experimental import pallas as pl
from jax.experimental.pallas import tpu as pltpu
from jax.sharding import PartitionSpec as P

NOPE = 64
ROPE = 32
VDIM = 64
QRANK = 768
KVRANK = 256
HEAD = NOPE + ROPE
PAIR = NOPE + VDIM

depth_scale = 1.4 / math.sqrt(62.0)
eps_value = 1e-05
masked_value = -1e30
score_scale = 1.0 / math.sqrt(NOPE + ROPE)
log2_scale = score_scale / math.log(2.0)

f32 = jnp.float32
bf16 = jnp.bfloat16


def contract(left, right, left_dim, right_dim):
    return lax.dot_general(
        left, right, (((left_dim,), (right_dim,)), ((), ())), preferred_element_type=f32
    )


def rms_norm(values, gain, axis=0):
    factor = lax.rsqrt(jnp.mean(values * values, axis=axis, keepdims=True) + eps_value)
    gain = gain[:, None] if axis == 0 else gain
    return (values * factor * gain, factor)


def rms_back(grad_out, values, factor, gain, axis=0):
    normed = values * factor
    scaled = grad_out * (gain[:, None] if axis == 0 else gain)
    grad_in = factor * (scaled - normed * jnp.mean(scaled * normed, axis=axis, keepdims=True))
    return (grad_in, jnp.sum(grad_out * normed, axis=axis + 1))


def angles(places, width):
    half_width = width // 2
    spectrum = 10000.0 ** (-2.0 * jnp.arange(half_width, dtype=jnp.float32) / width)
    turned = spectrum[:, None] * places.astype(jnp.float32)[None, :]
    return (jnp.cos(turned), jnp.sin(turned))


def rotate(values, cosine, sine):
    half = values.shape[0] // 2
    former, latter = values[:half], values[half:]
    return jnp.concatenate(
        [former * cosine - latter * sine, latter * cosine + former * sine], axis=0
    )


def unrotate(values, cosine, sine):
    half = values.shape[0] // 2
    former, latter = values[:half], values[half:]
    return jnp.concatenate(
        [former * cosine + latter * sine, latter * cosine - former * sine], axis=0
    )


def joined_keys(pairs, rotary):
    lane = lax.broadcasted_iota(jnp.int32, pairs.shape, 1)
    return jnp.where(lane < NOPE, pairs, rotary)


def attend_kernel(blocks, span, own, places, query_raw, cosine, sine, pairs, rotary, out, query_out, log_out, top, total, acc):
    half = ROPE // 2
    former = query_raw[NOPE : NOPE + half, :]
    latter = query_raw[NOPE + half :, :]
    query = jnp.concatenate(
        [
            query_raw[:NOPE, :],
            former * cosine[...] - latter * sine[...],
            latter * cosine[...] + former * sine[...],
        ],
        axis=0,
    ).astype(bf16)
    query_out[...] = query
    top[...] = jnp.full(top.shape, masked_value, f32)
    total[...] = jnp.zeros(total.shape, f32)
    acc[...] = jnp.zeros(acc.shape, f32)
    mine = places[own]

    def visit(block, diagonal):
        rows = pl.ds(block * span, span)
        pair = pairs[rows, :]
        key = joined_keys(pair, rotary[rows, :])[:, :HEAD]
        scores = contract(key, query, 1, 0)
        if diagonal:
            key_at = lax.broadcasted_iota(jnp.int32, scores.shape, 0)
            query_at = lax.broadcasted_iota(jnp.int32, scores.shape, 1)
            scores = jnp.where(key_at <= query_at, scores, masked_value)
        before = top[...]
        highest = jnp.maximum(before, jnp.max(scores, axis=0, keepdims=True))
        expo = jnp.exp2((scores - highest) * log2_scale)
        shrink = jnp.exp2((before - highest) * log2_scale)
        top[...] = highest
        total[...] = total[...] * shrink + jnp.sum(expo, axis=0, keepdims=True)
        acc[...] = acc[...] * shrink + contract(pair, expo.astype(bf16), 0, 0)

    for block in range(blocks):
        theirs = places[block]
        pl.when(theirs < mine)(lambda block=block: visit(block, False))
        pl.when(theirs == mine)(lambda block=block: visit(block, True))
    out[...] = (acc[NOPE:, :] / total[...]).astype(bf16)
    log_out[0] = top[...] * log2_scale + jnp.log2(total[...])


def attend(own, places, query_raw, cosine, sine, pairs, rotary):
    rows, tokens = query_raw.shape
    heads = rows // HEAD
    keys = pairs.shape[0]
    span = tokens
    blocks = keys // span
    elements = heads * tokens * keys
    half = ROPE // 2

    def kernel(*refs):
        attend_kernel(blocks, span, own, *refs)

    return pl.pallas_call(
        kernel,
        out_shape=(
            jax.ShapeDtypeStruct((heads * VDIM, tokens), bf16),
            jax.ShapeDtypeStruct((rows, tokens), bf16),
            jax.ShapeDtypeStruct((heads, 1, tokens), f32),
        ),
        grid_spec=pltpu.PrefetchScalarGridSpec(
            num_scalar_prefetch=1,
            grid=(heads,),
            in_specs=[
                pl.BlockSpec((HEAD, tokens), lambda h, p: (h, 0)),
                pl.BlockSpec((half, tokens), lambda h, p: (0, 0)),
                pl.BlockSpec((half, tokens), lambda h, p: (0, 0)),
                pl.BlockSpec((keys, PAIR), lambda h, p: (0, h)),
                pl.BlockSpec((keys, PAIR), lambda h, p: (0, 0)),
            ],
            out_specs=(
                pl.BlockSpec((VDIM, tokens), lambda h, p: (h, 0)),
                pl.BlockSpec((HEAD, tokens), lambda h, p: (h, 0)),
                pl.BlockSpec((1, 1, tokens), lambda h, p: (h, 0, 0)),
            ),
            scratch_shapes=[
                pltpu.VMEM((1, tokens), f32),
                pltpu.VMEM((1, tokens), f32),
                pltpu.VMEM((PAIR, tokens), f32),
            ],
        ),
        compiler_params=pltpu.CompilerParams(vmem_limit_bytes=32 * 1024 * 1024),
        cost_estimate=pl.CostEstimate(
            flops=4 * elements * 128, bytes_accessed=keys * heads * PAIR * 2, transcendentals=elements
        ),
        name="attend",
    )(places, query_raw, cosine, sine, pairs, rotary)


def attend_back_kernel(blocks, span, start, own, places, query_in, cosine, sine, pairs, rotary, grad_in, out_in, log_in, *rest):
    if start:
        base, query_grad, pair_grad, rotary_grad, acc = rest
    else:
        query_grad, pair_grad, rotary_grad, acc = rest
    half = ROPE // 2
    mine = places[own]
    query = query_in[...]
    grad = grad_in[...]
    inner = jnp.sum(grad.astype(f32) * out_in[...].astype(f32), axis=0, keepdims=True)
    grad_tall = jnp.concatenate([jnp.zeros((NOPE, grad.shape[1]), bf16), grad], axis=0)
    query_tall = jnp.concatenate([query, jnp.zeros((PAIR - HEAD, grad.shape[1]), bf16)], axis=0)
    log_total = log_in[0]
    acc[...] = jnp.zeros(acc.shape, f32)

    @pl.when(pl.program_id(0) == 0)
    def _():
        rotary_grad[...] = jnp.zeros(rotary_grad.shape, f32)

    def visit(block, diagonal):
        rows = pl.ds(block * span, span)
        pair = pairs[rows, :]
        key = joined_keys(pair, rotary[rows, :])
        scores = contract(key, query_tall, 1, 0)
        probs = jnp.exp2(scores * log2_scale - log_total)
        if diagonal:
            key_at = lax.broadcasted_iota(jnp.int32, scores.shape, 0)
            query_at = lax.broadcasted_iota(jnp.int32, scores.shape, 1)
            probs = jnp.where(key_at <= query_at, probs, 0.0)
        grad_probs = contract(pair, grad_tall, 1, 0)
        grad_scores = (probs * (grad_probs - inner)).astype(bf16)
        key_part = contract(grad_scores, query_tall, 1, 1) * score_scale
        value_part = contract(probs.astype(bf16), grad_tall, 1, 1)
        lane = lax.broadcasted_iota(jnp.int32, key_part.shape, 1)
        both = jnp.where(lane < NOPE, key_part, value_part)
        if start:
            both = both + base[rows, :].astype(f32)
        pair_grad[rows, :] = both.astype(bf16)
        rotary_grad[rows, :] += key_part
        acc[...] += contract(key, grad_scores, 0, 0)

    def skip(block):
        rows = pl.ds(block * span, span)
        if start:
            pair_grad[rows, :] = base[rows, :]
        else:
            pair_grad[rows, :] = jnp.zeros((span, PAIR), bf16)

    for block in range(blocks):
        theirs = places[block]
        pl.when(theirs < mine)(lambda block=block: visit(block, False))
        pl.when(theirs == mine)(lambda block=block: visit(block, True))
        pl.when(theirs > mine)(lambda block=block: skip(block))
    total = acc[...] * score_scale
    former = total[NOPE : NOPE + half, :]
    latter = total[NOPE + half : HEAD, :]
    query_grad[...] = jnp.concatenate(
        [
            total[:NOPE, :],
            former * cosine[...] + latter * sine[...],
            latter * cosine[...] - former * sine[...],
        ],
        axis=0,
    ).astype(bf16)


def attend_back(own, places, query, cosine, sine, pairs, rotary, grad, out, log_total, base):
    rows, tokens = query.shape
    heads = rows // HEAD
    keys = pairs.shape[0]
    span = tokens
    blocks = keys // span
    elements = heads * tokens * keys
    half = ROPE // 2
    start = base is not None

    def kernel(*refs):
        attend_back_kernel(blocks, span, start, own, *refs)

    args = [places, query, cosine, sine, pairs, rotary, grad, out, log_total]
    in_specs = [
        pl.BlockSpec((HEAD, tokens), lambda h, p: (h, 0)),
        pl.BlockSpec((half, tokens), lambda h, p: (0, 0)),
        pl.BlockSpec((half, tokens), lambda h, p: (0, 0)),
        pl.BlockSpec((keys, PAIR), lambda h, p: (0, h)),
        pl.BlockSpec((keys, PAIR), lambda h, p: (0, 0)),
        pl.BlockSpec((VDIM, tokens), lambda h, p: (h, 0)),
        pl.BlockSpec((VDIM, tokens), lambda h, p: (h, 0)),
        pl.BlockSpec((1, 1, tokens), lambda h, p: (h, 0, 0)),
    ]
    if start:
        args.append(base)
        in_specs.append(pl.BlockSpec((keys, PAIR), lambda h, p: (0, h)))
    return pl.pallas_call(
        kernel,
        out_shape=(
            jax.ShapeDtypeStruct((rows, tokens), bf16),
            jax.ShapeDtypeStruct((keys, heads * PAIR), bf16),
            jax.ShapeDtypeStruct((keys, PAIR), f32),
        ),
        grid_spec=pltpu.PrefetchScalarGridSpec(
            num_scalar_prefetch=1,
            grid=(heads,),
            in_specs=in_specs,
            out_specs=(
                pl.BlockSpec((HEAD, tokens), lambda h, p: (h, 0)),
                pl.BlockSpec((keys, PAIR), lambda h, p: (0, h)),
                pl.BlockSpec((keys, PAIR), lambda h, p: (0, 0)),
            ),
            scratch_shapes=[pltpu.VMEM((PAIR, tokens), f32)],
        ),
        compiler_params=pltpu.CompilerParams(vmem_limit_bytes=32 * 1024 * 1024),
        cost_estimate=pl.CostEstimate(
            flops=10 * elements * 128, bytes_accessed=keys * heads * PAIR * 4, transcendentals=elements
        ),
        name="attend_back",
    )(*args)


def ffn_front(normed, grad, weights, tile=256):
    tokens, width = normed.shape
    owners, kinds, rows, units = weights.shape

    def kernel(normed, grad, gate, up, down, hidden, grad_gate, grad_up):
        def product(left, weight):
            weight = weight[...].reshape(width, tile)
            return jnp.dot(left[...], weight, preferred_element_type=f32)

        gate_value = product(normed, gate)
        up_value = product(normed, up)
        grad_hidden = product(grad, down)
        sigma = jax.nn.sigmoid(gate_value)
        silu_gate = gate_value * sigma
        hidden[...] = (silu_gate * up_value).astype(bf16)
        slope = sigma * (1.0 + gate_value * (1.0 - sigma))
        grad_gate[...] = (grad_hidden * up_value * slope).astype(bf16)
        grad_up[...] = (grad_hidden * silu_gate).astype(bf16)

    whole = pl.BlockSpec((tokens, width), lambda n: (0, 0))
    weight = [
        pl.BlockSpec((owners, None, rows, tile), lambda n, kind=kind: (0, kind, 0, n))
        for kind in range(kinds)
    ]
    given = jax.ShapeDtypeStruct((tokens, units), bf16)
    block = pl.BlockSpec((tokens, tile), lambda n: (0, n))
    return pl.pallas_call(
        kernel,
        out_shape=(given, given, given),
        grid=(pl.cdiv(units, tile),),
        in_specs=[whole, whole] + weight,
        out_specs=(block, block, block),
        compiler_params=pltpu.CompilerParams(vmem_limit_bytes=40 * 1024 * 1024),
        cost_estimate=pl.CostEstimate(
            flops=6 * tokens * width * units,
            bytes_accessed=6 * width * units,
            transcendentals=tokens * units,
        ),
        name="ffn_front",
    )(normed, grad, weights, weights, weights)


def owners_at_once(rows):
    step = 1
    while step * rows % 128:
        step += 1
    return step


def rows_product(lefts, weights, kinds):
    tokens, units = lefts[0].shape
    owners, _, rows, _ = weights.shape
    step = owners_at_once(rows)
    tile = step * rows
    width = owners * rows
    count = len(lefts)

    def kernel(*refs):
        total = None
        for i in range(count):
            weight = refs[count + i][...].reshape(tile, units)
            part = contract(refs[i][...], weight, 1, 1)
            total = part if total is None else total + part
        refs[-1][...] = total.astype(bf16)

    whole = pl.BlockSpec((tokens, units), lambda n: (0, 0))
    weight = [
        pl.BlockSpec((step, None, rows, units), lambda n, kind=kind: (n, kind, 0, 0))
        for kind in kinds
    ]
    return pl.pallas_call(
        kernel,
        out_shape=jax.ShapeDtypeStruct((tokens, width), bf16),
        grid=(width // tile,),
        in_specs=[whole] * count + weight,
        out_specs=pl.BlockSpec((tokens, tile), lambda n: (0, n)),
        compiler_params=pltpu.CompilerParams(vmem_limit_bytes=40 * 1024 * 1024),
        cost_estimate=pl.CostEstimate(
            flops=2 * count * tokens * width * units,
            bytes_accessed=2 * count * width * units,
            transcendentals=0,
        ),
        name="rows_product",
    )(*lefts, *([weights] * count))


def weight_grads(groups, owners):
    lefts = []
    for left, _ in groups:
        if not any(left is other for other in lefts):
            lefts.append(left)
    which = [[left is other for other in lefts].index(True) for left, _ in groups]
    parts = len(lefts[0])
    tokens, width = lefts[0][0].shape
    units = groups[0][1][0].shape[1]
    count = len(groups)
    rows = width // owners
    step = owners_at_once(rows)
    tile = step * rows

    def kernel(*refs):
        left = refs[: parts * len(lefts)]
        right = refs[parts * len(lefts) : -1]
        out = refs[-1]
        for g in range(count):
            total = None
            for p in range(parts):
                part = contract(
                    left[which[g] * parts + p][...], right[g * parts + p][...], 0, 0
                )
                total = part if total is None else total + part
            out[:, g] = total.astype(bf16).reshape(step, rows, units)

    left_spec = pl.BlockSpec((tokens, tile), lambda n: (0, n))
    right_spec = pl.BlockSpec(
        (tokens, units), lambda n: (0, 0), pipeline_mode=pl.Buffered(buffer_count=1)
    )
    return pl.pallas_call(
        kernel,
        out_shape=jax.ShapeDtypeStruct((owners, count, rows, units), bf16),
        grid=(width // tile,),
        in_specs=[left_spec] * (parts * len(lefts)) + [right_spec] * (parts * count),
        out_specs=pl.BlockSpec((step, count, rows, units), lambda n: (n, 0, 0, 0)),
        compiler_params=pltpu.CompilerParams(vmem_limit_bytes=44 * 1024 * 1024),
        cost_estimate=pl.CostEstimate(
            flops=2 * parts * count * tokens * width * units,
            bytes_accessed=2 * (parts * count * tokens + count * width) * units,
            transcendentals=0,
        ),
        name="weight_grads",
    )(*[part for left in lefts for part in left], *[part for _, right in groups for part in right])


def pack_ups(output, query, latent):
    lanes = output.shape[1]
    rest = query[:, lanes:]
    rest = jnp.pad(rest, ((0, 0), (0, lanes - rest.shape[1])))
    return jnp.concatenate(
        [output, query[:, :lanes], rest, latent[:, :lanes], latent[:, lanes:]], axis=0
    )


def unpack_ups(packed, output_shape, query_shape, latent_shape):
    lanes = output_shape[1]
    at = output_shape[0]
    query_rows, latent_rows = query_shape[0], latent_shape[0]
    output = packed[..., :at, :]
    query = jnp.concatenate(
        [
            packed[..., at : at + query_rows, :],
            packed[..., at + query_rows : at + 2 * query_rows, : query_shape[1] - lanes],
        ],
        axis=-1,
    )
    at += 2 * query_rows
    latent = jnp.concatenate(
        [packed[..., at : at + latent_rows, :], packed[..., at + latent_rows :, :]], axis=-1
    )
    return output, query, latent


def ups_grads(grad_attn, attended, query_normed, query_grads, latent, pair_grad, owners):
    parts = len(grad_attn)
    tokens, width = grad_attn[0].shape
    lanes = attended[0].shape[0]
    rows, query_rows, latent_rows = (
        size // owners for size in (width, query_normed.shape[0], latent.shape[0])
    )
    columns = query_grads[0].shape[0]
    step = owners_at_once(rows)
    all_rows = rows + 2 * query_rows + 2 * latent_rows
    keys = latent.shape[1]

    def kernel(*refs):
        grads, refs = refs[:parts], refs[parts:]
        outs, refs = refs[:parts], refs[parts:]
        normed, refs = refs[0], refs[1:]
        queries, refs = refs[:parts], refs[parts:]
        latent, pairs, out = refs
        total, query = None, None
        for i in range(parts):
            part = contract(grads[i][...], outs[i][...], 0, 1)
            total = part if total is None else total + part
            part = contract(normed[:, i * tokens : (i + 1) * tokens], queries[i][...], 1, 1)
            query = part if query is None else query + part
        out[:, :rows, :] = total.astype(bf16).reshape(step, rows, lanes)
        query = query.astype(bf16).reshape(step, query_rows, columns)
        at = rows
        out[:, at : at + query_rows, :] = query[:, :, :lanes]
        at += query_rows
        out[:, at : at + query_rows, : columns - lanes] = query[:, :, lanes:]
        out[:, at : at + query_rows, columns - lanes :] = jnp.zeros(
            (step, query_rows, 2 * lanes - columns), bf16
        )
        at += query_rows
        both = jnp.dot(latent[...], pairs[...], preferred_element_type=f32)
        both = both.astype(bf16).reshape(step, latent_rows, 2 * lanes)
        out[:, at : at + latent_rows, :] = both[:, :, :lanes]
        at += latent_rows
        out[:, at : at + latent_rows, :] = both[:, :, lanes:]

    def fixed(shape):
        return pl.BlockSpec(shape, lambda n: (0, 0))

    return pl.pallas_call(
        kernel,
        out_shape=jax.ShapeDtypeStruct((owners, all_rows, lanes), bf16),
        grid=(owners // step,),
        in_specs=[pl.BlockSpec((tokens, step * rows), lambda n: (0, n))] * parts
        + [fixed((lanes, tokens))] * parts
        + [pl.BlockSpec((step * query_rows, parts * tokens), lambda n: (n, 0))]
        + [fixed((columns, tokens))] * parts
        + [pl.BlockSpec((step * latent_rows, keys), lambda n: (n, 0)), fixed(pair_grad.shape)],
        out_specs=pl.BlockSpec((step, all_rows, lanes), lambda n: (n, 0, 0)),
        compiler_params=pltpu.CompilerParams(vmem_limit_bytes=40 * 1024 * 1024),
        cost_estimate=pl.CostEstimate(
            flops=2 * parts * tokens * (width * lanes + query_normed.shape[0] * columns)
            + 4 * keys * latent.shape[0] * lanes,
            bytes_accessed=2 * (owners * all_rows * lanes + keys * lanes * 2),
            transcendentals=0,
        ),
        name="ups_grads",
    )(*grad_attn, *attended, query_normed, *query_grads, latent, pair_grad)


def held(*values):
    out = lax.optimization_barrier(values)
    return out if len(values) > 1 else out[0]


class Order:
    def __init__(self):
        self.last = None

    def take(self, *values):
        if self.last is not None:
            values = lax.optimization_barrier((*values, self.last))[:-1]
        return values if len(values) > 1 else values[0]

    def mark(self, value):
        self.last = value
        return value


def low_sum_of(left, right):
    return (left.astype(f32) + right.astype(f32)).astype(bf16)


class LinePipe:
    def __init__(self, order):
        self.order = order
        self.direct = lax.axis_size("tensor") != 4
        index = lax.axis_index("tensor")
        self.inner = (index == 1) | (index == 2)
        self.waiting = []
        self.entered = None
        self.crossed = None
        self.left = None
        self.sums = {}
        self.count = 0

    def push(self, part, pieces, ahead=False):
        rows = part.shape[0] // pieces
        keys = []
        fresh = []
        for i in range(pieces):
            piece = part[i * rows : (i + 1) * rows]
            keys.append(self.count)
            if self.direct:
                total = lax.psum(piece, "tensor")
                self.sums[self.count] = (total, total)
            else:
                fresh.append((self.count, piece))
            self.count += 1
        self.waiting = fresh + self.waiting if ahead else self.waiting + fresh
        return keys

    def step(self, *others):
        if self.direct:
            return others if len(others) != 1 else others[0]
        arrived = []
        if self.entered is not None:
            arrived += [self.entered[1], self.entered[2]]
        if self.crossed is not None:
            arrived += [self.crossed[1], self.crossed[2]]
        fresh = self.waiting.pop(0) if self.waiting else None
        if fresh is not None:
            arrived.append(fresh[1])
        if self.left is not None:
            others = others + (self.left,)
        if not arrived and not others:
            return None
        taken = self.order.take(*arrived, *others)
        if len(arrived) + len(others) == 1:
            taken = (taken,)
        taken = list(taken)
        if self.left is not None:
            taken.pop()
        half = whole = None
        if self.entered is not None:
            half = low_sum_of(taken.pop(0), taken.pop(0))
        if self.crossed is not None:
            whole = low_sum_of(taken.pop(0), taken.pop(0))
        low = taken.pop(0) if fresh is not None else None
        joint = whole is not None and low is not None and whole.shape == low.shape
        sends = [value for value in (half, whole) if value is not None]
        if joint:
            sends.append(jnp.where(self.inner, whole, low))
        elif low is not None:
            sends.append(low)
        if sends:
            sends = lax.optimization_barrier(tuple(sends))
            self.order.mark(sends[-1])
        sends = list(sends)
        half = sends.pop(0) if half is not None else None
        whole = sends.pop(0) if whole is not None else None
        crossed, entered, left = None, None, None
        inwards, outwards = [(0, 1), (3, 2)], [(1, 0), (2, 3)]
        if joint:
            got = lax.ppermute(sends[0], "tensor", inwards + outwards)
            self.sums[self.crossed[0]] = (whole, got)
            entered = (fresh[0], sends[0], got)
        else:
            if whole is not None:
                got = left = lax.ppermute(whole, "tensor", outwards)
                self.sums[self.crossed[0]] = (whole, got)
            if low is not None:
                entered = (fresh[0], sends[0], lax.ppermute(sends[0], "tensor", inwards))
        if joint:
            entered = (fresh[0], low, got)
        if half is not None:
            crossed = (self.entered[0], half, lax.ppermute(half, "tensor", [(1, 2), (2, 1)]))
        self.entered, self.crossed, self.left = entered, crossed, left
        return taken if len(taken) != 1 else taken[0]

    def done(self, keys):
        pieces = [jnp.where(self.inner, *self.sums[key]) for key in keys]
        return jnp.concatenate(pieces, axis=0)


def direct_sum(order, part):
    count = lax.axis_size("tensor")
    if count != 4:
        total = lax.psum(part, "tensor")
        return lambda: total
    index = lax.axis_index("tensor")
    rows = part.shape[0] // count

    def share(k):
        return lax.dynamic_slice_in_dim(part, (index + k) % count * rows, rows, 0)

    shares = held(*[share(k) for k in range(count)])
    order.mark(shares[1])
    got = [
        lax.ppermute(shares[k], "tensor", [(i, (i + k) % count) for i in range(count)])
        for k in (2, 1, 3)
    ]

    def finish():
        mine = order.take(shares[0], *got)
        mine = sum(value.astype(f32) for value in mine).astype(bf16)
        mine = order.mark(held(mine))
        pieces = [mine] + [
            lax.ppermute(mine, "tensor", [((i + k) % count, i) for i in range(count)])
            for k in range(1, count)
        ]
        twice = jnp.concatenate(pieces + pieces, axis=0)
        start = (count - index) % count * rows
        return lax.dynamic_slice_in_dim(twice, start, count * rows, 0)

    return finish


def from_others(rows):
    count = lax.axis_size("ctx")
    return [
        lax.ppermute(rows, "ctx", [((i + k) % count, i) for i in range(count)])
        for k in range(1, count)
    ]


def back_to_owners(blocks):
    count = lax.axis_size("ctx")
    total = blocks[0].astype(f32)
    for k in range(1, count):
        total = total + lax.ppermute(
            blocks[k], "ctx", [(i, (i + k) % count) for i in range(count)]
        ).astype(f32)
    return total


def per_device(
    layer_input,
    cotangent,
    span_order,
    query_down,
    latent_down,
    query_up,
    latent_up,
    output_weight,
    gate_weight,
    up_weight,
    down_weight,
    first_gain,
    query_gain,
    latent_gain,
    second_gain,
):
    ctx_count = lax.axis_size("ctx")
    tensor_count = lax.axis_size("tensor")
    ctx_index = lax.axis_index("ctx")
    part_index = lax.axis_index("tensor")
    tokens = layer_input.shape[1]
    spans = span_order.shape[0] // ctx_count
    span = tokens // spans
    width = layer_input.shape[2]
    chunks = [slice(i * span, (i + 1) * span) for i in range(spans)]
    weights_at = ("dp", "ctx")
    order = Order()

    owners = weights_count()
    down_both = lax.all_gather(
        jnp.concatenate([query_down, latent_down], axis=1), weights_at, axis=0, tiled=True
    )
    inputs = layer_input[0]
    normed_one, factor_one = rms_norm(inputs.astype(f32), first_gain, -1)
    norm_one = normed_one.astype(bf16)
    output_rows = output_weight.T
    shapes = [output_rows.shape, query_up.shape, latent_up.shape]
    ups = pack_ups(output_rows, query_up, latent_up)
    ups, norm_one = held(ups, norm_one)
    ups = lax.all_gather(ups, weights_at, axis=0)

    places = lax.dynamic_slice_in_dim(
        jnp.concatenate([span_order, span_order]), ctx_index * spans, spans * ctx_count
    )
    local_places = (
        places[:spans, None] * span + jnp.arange(span, dtype=jnp.int32)[None, :]
    ).reshape(-1)
    cosine, sine = angles(local_places, ROPE)

    lowered = contract(down_both, norm_one, 0, 1)
    ffn_weights = jnp.stack([gate_weight, up_weight, down_weight.T])
    ffn_weights, lowered = held(ffn_weights, lowered)
    ffn_weights = lax.all_gather(ffn_weights, weights_at, axis=0)
    query_latent = lowered[:QRANK]
    latent_raw = lowered[QRANK : QRANK + KVRANK]
    latent_normed, latent_factor = rms_norm(latent_raw, latent_gain)
    rotary_key = rotate(lowered[QRANK + KVRANK :], cosine, sine)
    latent_pack = jnp.concatenate([latent_normed, rotary_key], axis=0).astype(bf16)
    ups, _ = held(ups, latent_pack)
    sequence_pack = jnp.concatenate([latent_pack] + from_others(latent_pack), axis=1)
    output_all, query_up_all, latent_up_all = [
        part.reshape(-1, part.shape[-1]) for part in unpack_ups(ups, *shapes)
    ]
    query_normed, query_factor = rms_norm(query_latent, query_gain)
    query_normed = query_normed.astype(bf16)
    query_raw = contract(query_up_all, query_normed, 0, 0)
    sequence_latent = sequence_pack[:KVRANK]
    pairs = contract(sequence_latent, latent_up_all, 0, 0).astype(bf16)
    rotary = jnp.pad(sequence_pack[KVRANK:].T, ((0, 0), (NOPE, PAIR - HEAD)))

    grad_ffn = (depth_scale * cotangent[0].astype(f32)).astype(bf16)
    pipe = LinePipe(order)
    attended, queries, log_totals = [], [], []
    attn_sums = []
    for i, rows in enumerate(chunks):
        raw = order.take(query_raw[:, rows])
        out, query, log_total = attend(
            i, places, raw, cosine[:, rows], sine[:, rows], pairs, rotary
        )
        order.mark(out)
        attended.append(out)
        queries.append(query)
        log_totals.append(log_total)
        if i > 0:
            pipe.step()
        part = contract(order.take(out), output_all, 0, 1).astype(bf16)
        attn_sums.append(pipe.push(order.mark(held(part)), 2))
        pipe.step()
    pipe.step()

    def ffn_start(i, rows):
        total = order.take(pipe.done(attn_sums[i]))
        middle = inputs[rows].astype(f32) + depth_scale * total.astype(f32)
        normed_two, factor = rms_norm(middle, second_gain, -1)
        norm_two = order.mark(held(normed_two.astype(bf16)))
        hidden, grad_gate, grad_up = ffn_front(norm_two, grad_ffn[rows], ffn_weights)
        order.mark(hidden)
        return middle, factor, norm_two, hidden, grad_gate, grad_up

    def ffn_end(parts):
        grad_gate, grad_up = order.take(parts[4], parts[5])
        part = rows_product([grad_gate, grad_up], ffn_weights, [0, 1])
        return pipe.push(order.mark(part), 2)

    def reduced(grad):
        return lax.psum_scatter(grad, weights_at, scatter_dimension=0, tiled=grad.ndim == 2)

    def ffn_out(i):
        part = rows_product([order.take(hidden[i])], ffn_weights, [2])
        return order.mark(part)

    mine = ffn_start(0, chunks[0])
    hidden = [mine[3]]
    pipe.step()
    norm_sums = [ffn_end(mine)]
    pipe.step()
    ffn_parts = [ffn_out(0)]
    pipe.step()
    theirs = ffn_start(1, chunks[1])
    pipe.step()
    norm_sums.append(ffn_end(theirs))
    pipe.step()
    middle, factor_two, norm_two, hidden, grad_gate, grad_up = zip(mine, theirs)
    ffn_cots = [order.take(grad_ffn[rows]) for rows in chunks]
    ffn_grads = weight_grads(
        [(norm_two, grad_gate), (norm_two, grad_up), (ffn_cots, hidden)], owners
    )
    order.mark(ffn_grads)
    pipe.step()
    ffn_done = reduced(order.take(ffn_grads))
    ffn_sums = [pipe.push(ffn_parts[0], 2)]

    grad_middle, grad_attn, second_parts = [], [], []
    query_grads, pair_grad, rotary_grad = [], None, 0.0
    for i, rows in enumerate(chunks):
        total = order.take(pipe.done(norm_sums[i]))
        middle_part, second_part = rms_back(
            total.astype(f32), middle[i], factor_two[i], second_gain, -1
        )
        second_parts.append(second_part)
        grad_middle.append(cotangent[0, rows].astype(f32) + middle_part)
        grad_attn.append(held((depth_scale * grad_middle[i]).astype(bf16)))
        order.mark(grad_attn[i])
        grad_attended = contract(output_all, grad_attn[i], 0, 1).astype(bf16)
        query_grad, pair_grad, rotary_part = attend_back(
            i,
            places,
            queries[i],
            cosine[:, rows],
            sine[:, rows],
            pairs,
            rotary,
            grad_attended,
            attended[i],
            log_totals[i],
            pair_grad,
        )
        order.mark(query_grad)
        query_grads.append(query_grad)
        rotary_grad = rotary_grad + rotary_part[:, NOPE:HEAD]
        if i == 0:
            pipe.step()
            ffn_parts.append(ffn_out(1))
            ffn_sums.append(pipe.push(ffn_parts[1], 2))
            pipe.step()
            pipe.step()
    second_gain_grad = sum(second_parts)

    pack_grad = jnp.concatenate(
        [contract(latent_up_all, pair_grad, 1, 1), rotary_grad.T], axis=0
    ).astype(bf16)
    pack_local = back_to_owners(
        [pack_grad[:, k * tokens : (k + 1) * tokens] for k in range(ctx_count)]
    )
    query_part = contract(query_up_all, jnp.concatenate(query_grads, axis=1), 1, 0)
    low_part = jnp.concatenate([query_part, pack_local], axis=0).astype(bf16)
    low_part = order.mark(held(order.take(low_part)))
    low_finish = direct_sum(order, low_part)
    outs_grad = ups_grads(
        [order.take(part) for part in grad_attn],
        attended,
        query_normed,
        query_grads,
        sequence_latent,
        pair_grad,
        owners,
    )
    order.mark(outs_grad)
    low_sums = low_finish()
    outs_grad, ffn_done = order.take(outs_grad, ffn_done)
    outs_done = reduced(outs_grad)
    pipe.step()
    both = order.take(low_sums).astype(f32)
    grad_query_latent, query_gain_grad = rms_back(
        both[:QRANK], query_latent, query_factor, query_gain
    )
    grad_latent_normed, latent_gain_grad = rms_back(
        both[QRANK : QRANK + KVRANK], latent_raw, latent_factor, latent_gain
    )
    lowered_grad = jnp.concatenate(
        [grad_query_latent, grad_latent_normed, unrotate(both[QRANK + KVRANK :], cosine, sine)],
        axis=0,
    ).astype(bf16)
    lowered_grad = order.mark(held(lowered_grad))
    outs_done = pipe.step(outs_done)
    query_cols = QRANK // tensor_count
    latent_cols = (KVRANK + ROPE) // tensor_count
    cut = jnp.concatenate(
        [
            lax.dynamic_slice_in_dim(lowered_grad, part_index * query_cols, query_cols, 0),
            lax.dynamic_slice_in_dim(
                lowered_grad, QRANK + part_index * latent_cols, latent_cols, 0
            ),
        ],
        axis=0,
    )
    down_cut = contract(norm_one, cut, 0, 1)
    grad_norm_one = contract(lowered_grad, down_both, 0, 1)
    _, first_gain_grad = rms_back(
        grad_norm_one, inputs.astype(f32), factor_one, first_gain, -1
    )
    gains = jnp.concatenate(
        [query_gain_grad.reshape(owners, -1), latent_gain_grad.reshape(owners, -1)], axis=1
    )
    gains = jnp.pad(gains, ((0, 0), (0, width // owners - gains.shape[1]))).reshape(-1)
    columns = [first_gain_grad[:, None], second_gain_grad[:, None], gains[:, None]]
    last = jnp.concatenate([down_cut] + columns, axis=1).astype(bf16)
    last = order.take(last)
    last_done = reduced(order.mark(last)).astype(f32)
    grad_norm_one = order.take(grad_norm_one)
    input_part, _ = rms_back(grad_norm_one, inputs.astype(f32), factor_one, first_gain, -1)
    input_rows = jnp.concatenate(grad_middle, axis=0) + input_part
    pipe.step()
    pipe.step()
    qd_done = last_done[:, :query_cols]
    ld_done = last_done[:, query_cols : query_cols + latent_cols]
    first_done = last_done[:, query_cols + latent_cols]
    second_done = last_done[:, query_cols + latent_cols + 1]
    gains_done = last_done[:, query_cols + latent_cols + 2]
    query_done = gains_done[: QRANK // owners]
    latent_done = gains_done[QRANK // owners : (QRANK + KVRANK) // owners]
    out_done, qu_done, lu_done = unpack_ups(outs_done.astype(f32), *shapes)
    out_done = out_done.T
    ffn_done = ffn_done.astype(f32)

    block_rows = [
        (middle[i] + depth_scale * pipe.done(ffn_sums[i]).astype(f32)).astype(bf16)
        for i in range(spans)
    ]
    return (
        jnp.concatenate(block_rows, axis=0)[None],
        input_rows[None],
        qd_done,
        ld_done,
        qu_done,
        lu_done,
        out_done,
        ffn_done[0],
        ffn_done[1],
        ffn_done[2].T,
        first_done,
        query_done,
        latent_done,
        second_done,
    )


def weights_count():
    return lax.axis_size("dp") * lax.axis_size("ctx")


def solution(mesh):
    placed = (
        P("dp", "ctx", None),
        P("dp", "ctx", None),
        P(),
        P(("dp", "ctx"), None),
        P(("dp", "ctx"), None),
        P(("dp", "ctx"), "tensor"),
        P(("dp", "ctx"), "tensor"),
        P("tensor", ("dp", "ctx")),
        P(("dp", "ctx"), "tensor"),
        P(("dp", "ctx"), "tensor"),
        P("tensor", ("dp", "ctx")),
        P(),
        P(),
        P(),
        P(),
    )
    return jax.shard_map(
        per_device,
        mesh=mesh,
        in_specs=placed,
        out_specs=(
            P("dp", "ctx", None),
            P("dp", "ctx", None),
            P(("dp", "ctx"), "tensor"),
            P(("dp", "ctx"), "tensor"),
            P(("dp", "ctx"), "tensor"),
            P(("dp", "ctx"), "tensor"),
            P("tensor", ("dp", "ctx")),
            P(("dp", "ctx"), "tensor"),
            P(("dp", "ctx"), "tensor"),
            P("tensor", ("dp", "ctx")),
            P(("dp", "ctx")),
            P(("dp", "ctx")),
            P(("dp", "ctx")),
            P(("dp", "ctx")),
        ),
        check_vma=False,
    )
```

profile of v0, /device:TPU:0, one launch (start us, length us, event | category | flops | bytes accessed | tf_op | source)
XLA Modules:
  0.0 735.2 jit_solution(6551785886308234661)
XLA Ops:
  23.4 33.7 %all-gather.6.cloned.1.call-done = bf16[2560,1056]{1,0:T(8,128)(2,1)} async-done(((bf16[320,1056]{1,0:T(8,128)(2,1)}), bf16[2560,1056]{1,0:T(8,128)(2,1)}) %all-gather.6.cloned.1.call-update) | async-done | bytes 5406736 | tf_op jit(solution)/shard_map/all_gather | solution.py:706
  57.1 10.4 %fusion.68 = f32[1056,768]{1,0:T(8,128)} fusion(bf16[2560,1056]{1,0:T(8,128)(2,1)} %all-gather.6.cloned.1.call-done, bf16[768,2560]{1,0:T(8,128)(2,1)} %fusion.4), kind=kOutput, calls=%fused_computation.220 | convolution fusion | flops 4152360960 | bytes 12582912 | tf_op jit(solution)/shard_map/dot_general | solution.py:29
  77.5 10.2 %collective-permute-done = bf16[288,768]{1,0:T(8,128)(2,1)S(1)} collective-permute-done((bf16[288,768]{1,0:T(8,128)(2,1)S(1)}, bf16[288,768]{1,0:T(8,128)(2,1)S(1)}, u32[]{:S(2)}, u32[]{:S(2)}) %collective-permute-start) | collective-permute-done | bytes 442400 | tf_op jit(solution)/shard_map/ppermute | solution.py:661
  90.1 16.5 %all-gather.8.cloned.1.call-done = bf16[4608,640]{1,0:T(8,128)(2,1)} async-done(((bf16[576,640]{1,0:T(8,128)(2,1)}), bf16[4608,640]{1,0:T(8,128)(2,1)}) %all-gather.8.cloned.1.call-update) | async-done | bytes 5898256 | tf_op jit(solution)/shard_map/all_gather | solution.py:716
  133.2 18.5 %attend.3 = (bf16[640,384]{1,0:T(8,128)(2,1)S(1)}, bf16[960,384]{1,0:T(8,128)(2,1)S(1)}, f32[10,1,384]{2,1,0:T(1,128)S(1)}) custom-call(s32[4]{0:T(128)S(1)} %dynamic_slice.24.refs_0_, f32[960,384]{1,0:T(8,128)S(1)} %get-tuple-element.171.refs_1_, f32[16,384]{1,0:T(8,128)S(1)} %get-tuple-element.386.refs_2_, f32[16,384]{1,0:T(8,128)S(1)} %get-tuple-element.377.refs_3_, ...), custom_call_target="tpu_custom_call" | custom-call | flops 3019898880 | bytes 3932160 | tf_op jit(solution)/shard_map/attend/pallas_call | solution.py:130
  160.5 17.9 %collective-permute-done.2 = bf16[192,2560]{1,0:T(8,128)(2,1)S(1)} collective-permute-done((bf16[192,2560]{1,0:T(8,128)(2,1)S(1)}, bf16[192,2560]{1,0:T(8,128)(2,1)S(1)}, u32[]{:S(2)}, u32[]{:S(2)}) %collective-permute-start.2) | collective-permute-done | bytes 983072 | tf_op jit(solution)/shard_map/ppermute | solution.py:612
  184.4 19.1 %collective-permute-done.4 = bf16[192,2560]{1,0:T(8,128)(2,1)S(1)} collective-permute-done((bf16[192,2560]{1,0:T(8,128)(2,1)S(1)}, bf16[192,2560]{1,0:T(8,128)(2,1)S(1)}, u32[]{:S(2)}, u32[]{:S(2)}) %collective-permute-start.4) | collective-permute-done | bytes 983072 | tf_op jit(solution)/shard_map/ppermute | solution.py:604
  213.4 15.2 %collective-permute-done.6 = bf16[192,2560]{1,0:T(8,128)(2,1)S(1)} collective-permute-done((bf16[192,2560]{1,0:T(8,128)(2,1)S(1)}, bf16[192,2560]{1,0:T(8,128)(2,1)S(1)}, u32[]{:S(2)}, u32[]{:S(2)}) %collective-permute-start.6) | collective-permute-done | bytes 983072 | tf_op jit(solution)/shard_map/ppermute | solution.py:604
  237.1 16.0 %ffn_front.2 = (bf16[384,1600]{1,0:T(8,128)(2,1)S(1)}, bf16[384,1600]{1,0:T(8,128)(2,1)S(1)}, bf16[384,1600]{1,0:T(8,128)(2,1)S(1)}) custom-call(bf16[384,2560]{1,0:T(8,128)(2,1)S(1)} %multiply_convert_fusion.4.normed.refs_0_, bf16[384,2560]{1,0:T(8,128)(2,1)S(1)} %copy-done.8, bf16[8,3,320,1600]{3,2,1,0:T(8,128)(2,1)} %bitcast.107, ...), custom_call_target="tpu_custom_call" | custom-call | flops 9437184000 | bytes 24576000 | tf_op jit(solution)/shard_map/ffn_front/pallas_call | solution.py:311
  257.2 11.6 %rows_product.4 = bf16[384,2560]{1,0:T(8,128)(2,1)S(1)} custom-call(bf16[384,1600]{1,0:T(8,128)(2,1)S(1)} %get-tuple-element.206.refs_0_.refs_4_, bf16[384,1600]{1,0:T(8,128)(2,1)S(1)} %get-tuple-element.207.refs_1_.refs_6_, bf16[8,3,320,1600]{3,2,1,0:T(8,128)(2,1)} %bitcast.110, bf16[8,3,320,1600]{3,2,1,0:T(8,128)(2,1)} %bitcast.111), custom_call_target="tpu_custom_call" | custom-call | flops 6291456000 | bytes 16384000 | tf_op jit(solution)/shard_map/rows_product/pallas_call | solution.py:355
  269.0 12.0 %collective-permute-done.9 = bf16[192,2560]{1,0:T(8,128)(2,1)S(1)} collective-permute-done((bf16[192,2560]{1,0:T(8,128)(2,1)S(1)}, bf16[192,2560]{1,0:T(8,128)(2,1)S(1)}, u32[]{:S(2)}, u32[]{:S(2)}) %collective-permute-start.9) | collective-permute-done | bytes 983072 | tf_op jit(solution)/shard_map/ppermute | solution.py:609
  293.1 14.1 %collective-permute-done.10 = bf16[192,2560]{1,0:T(8,128)(2,1)S(1)} collective-permute-done((bf16[192,2560]{1,0:T(8,128)(2,1)S(1)}, bf16[192,2560]{1,0:T(8,128)(2,1)S(1)}, u32[]{:S(2)}, u32[]{:S(2)}) %collective-permute-start.10) | collective-permute-done | bytes 983072 | tf_op jit(solution)/shard_map/ppermute | solution.py:604
  315.4 16.6 %ffn_front.3 = (bf16[384,1600]{1,0:T(8,128)(2,1)S(1)}, bf16[384,1600]{1,0:T(8,128)(2,1)S(1)}, bf16[384,1600]{1,0:T(8,128)(2,1)S(1)}) custom-call(bf16[384,2560]{1,0:T(8,128)(2,1)S(1)} %multiply_convert_fusion.3.normed.refs_1_, bf16[384,2560]{1,0:T(8,128)(2,1)S(1)} %copy-done.7, bf16[8,3,320,1600]{3,2,1,0:T(8,128)(2,1)} %bitcast.113, ...), custom_call_target="tpu_custom_call" | custom-call | flops 9437184000 | bytes 24576000 | tf_op jit(solution)/shard_map/ffn_front/pallas_call | solution.py:311
  336.3 11.6 %rows_product.6 = bf16[384,2560]{1,0:T(8,128)(2,1)S(1)} custom-call(bf16[384,1600]{1,0:T(8,128)(2,1)S(1)} %get-tuple-element.229.refs_0_.refs_5_, bf16[384,1600]{1,0:T(8,128)(2,1)S(1)} %get-tuple-element.230.refs_1_.refs_7_, bf16[8,3,320,1600]{3,2,1,0:T(8,128)(2,1)} %bitcast.116, bf16[8,3,320,1600]{3,2,1,0:T(8,128)(2,1)} %bitcast.117), custom_call_target="tpu_custom_call" | custom-call | flops 6291456000 | bytes 16384000 | tf_op jit(solution)/shard_map/rows_product/pallas_call | solution.py:355
  364.2 32.5 %weight_grads.1 = bf16[8,3,320,1600]{3,2,1,0:T(8,128)(2,1)} custom-call(bf16[384,2560]{1,0:T(8,128)(2,1)S(1)} %multiply_convert_fusion.4.normed.refs_0_, bf16[384,2560]{1,0:T(8,128)(2,1)} %copy-done.6, bf16[384,2560]{1,0:T(8,128)(2,1)} %get-tuple-element.235.grad.refs_2_, bf16[384,2560]{1,0:T(8,128)(2,1)} %get-tuple-element.236.grad.refs_3_, ...), custom_call_target="tpu_custom_call" | custom-call | flops 18874368000 | bytes 31948800 | tf_op jit(solution)/shard_map/weight_grads/pallas_call | solution.py:402
  462.8 13.5 %collective-permute-done.20 = bf16[192,2560]{1,0:T(8,128)(2,1)S(1)} collective-permute-done((bf16[192,2560]{1,0:T(8,128)(2,1)S(1)}, bf16[192,2560]{1,0:T(8,128)(2,1)S(1)}, u32[]{:S(2)}, u32[]{:S(2)}) %collective-permute-start.20) | collective-permute-done | bytes 983072 | tf_op jit(solution)/shard_map/ppermute | solution.py:604
  493.4 21.2 %attend_back.3 = (bf16[960,384]{1,0:T(8,128)(2,1)S(1)}, bf16[1536,1280]{1,0:T(8,128)(2,1)S(1)}, f32[1536,128]{1,0:T(8,128)S(1)}) custom-call(s32[4]{0:T(128)S(1)} %copy-done.39, bf16[960,384]{1,0:T(8,128)(2,1)S(1)} %copy-done.41, f32[16,384]{1,0:T(8,128)S(1)} %copy-done.33, f32[16,384]{1,0:T(8,128)S(1)} %copy-done.31, bf16[1536,1280]{1,0:T(8,128)(2,1)S(1)} %copy-done.3, ...), custom_call_target="tpu_custom_call" | custom-call | flops 7549747200 | bytes 7864320 | tf_op jit(solution)/shard_map/attend_back/pallas_call | solution.py:259
  533.7 14.4 %collective-permute-done.24 = bf16[288,768]{1,0:T(8,128)(2,1)S(1)} collective-permute-done((bf16[288,768]{1,0:T(8,128)(2,1)S(1)}, bf16[288,768]{1,0:T(8,128)(2,1)S(1)}, u32[]{:S(2)}, u32[]{:S(2)}) %collective-permute-start.24) | collective-permute-done | bytes 442400 | tf_op jit(solution)/shard_map/ppermute | solution.py:670
  555.6 10.6 %ups_grads.1 = bf16[8,576,640]{2,1,0:T(8,128)(2,1)} custom-call(bf16[384,2560]{1,0:T(8,128)(2,1)S(1)} %get-tuple-element.285.refs_0_, bf16[384,2560]{1,0:T(8,128)(2,1)S(1)} %copy-done.5, bf16[640,384]{1,0:T(8,128)(2,1)S(1)} %copy-done.23, bf16[640,384]{1,0:T(8,128)(2,1)S(1)} %copy-done.26, bf16[768,768]{1,0:T(8,128)(2,1)S(1)} %copy-done.12, ...), custom_call_target="tpu_custom_call" | custom-call | flops 4655677440 | bytes 9830400 | tf_op jit(solution)/shard_map/ups_grads/pallas_call | solution.py:489
  566.2 15.5 %collective-permute-done.25 = bf16[264,768]{1,0:T(8,128)(2,1)} collective-permute-done((bf16[264,768]{1,0:T(8,128)(2,1)}, bf16[264,768]{1,0:T(8,128)(2,1)}, u32[]{:S(2)}, u32[]{:S(2)}) %collective-permute-start.25) | collective-permute-done | bytes 405536 | tf_op jit(solution)/shard_map/ppermute | solution.py:639
  604.0 11.4 %collective-permute-done.30 = bf16[264,768]{1,0:T(8,128)(2,1)} collective-permute-done((bf16[264,768]{1,0:T(8,128)(2,1)S(1)}, bf16[264,768]{1,0:T(8,128)(2,1)}, u32[]{:S(2)}, u32[]{:S(2)}) %collective-permute-start.30) | collective-permute-done | bytes 405536 | tf_op jit(solution)/shard_map/ppermute | solution.py:648
  629.1 11.3 %fusion.5 = (bf16[2560]{0:T(1024)(128)(2,1)S(1)}, f32[768,2560]{1,0:T(8,128)}) fusion(bf16[1,768,2560]{2,1,0:T(8,128)(2,1)S(1)} %copy-done.48, f32[768]{0:T(1024)S(1)} %copy-done.112, bf16[1056,768]{1,0:T(8,128)(2,1)S(1)} %pad_maximum_fusion.6, bf16[2560,1056]{1,0:T(8,128)(2,1)} %all-gather.6.cloned.1.call-done), kind=kOutput, calls=%fused_computation.7 | convolution fusion | flops 4160222720 | bytes 18833408 | tf_op jit(solution)/shard_map/dot_general | solution.py:29
  670.2 11.1 %fusion.10 = f32[1,768,2560]{2,1,0:T(8,128)} fusion(f32[384,2560]{1,0:T(8,128)} %get-tuple-element.327, f32[384,2560]{1,0:T(8,128)} %get-tuple-element.335, f32[768,2560]{1,0:T(8,128)} %get-tuple-element.311, bf16[1,768,2560]{2,1,0:T(8,128)(2,1)} %param.15, f32[768]{0:T(1024)S(1)} %broadcast_multiply_fusion.2, f32[2560]{0:T(1024)S(1)} %copy-done.109, ...), kind=kLoop, calls=%fused_computation.12 | loop fusion | flops 15728640 | bytes 27541504 | tf_op jit(solution)/shard_map/broadcast_in_dim | solution.py:928
  692.0 27.4 %collective-permute-done.35 = bf16[192,2560]{1,0:T(8,128)(2,1)S(1)} collective-permute-done((bf16[192,2560]{1,0:T(8,128)(2,1)S(1)}, bf16[192,2560]{1,0:T(8,128)(2,1)S(1)}, u32[]{:S(2)}, u32[]{:S(2)}) %collective-permute-start.35) | collective-permute-done | bytes 983072 | tf_op jit(solution)/shard_map/ppermute | solution.py:609
  (507 shorter events, 326.1 us)
Async XLA Ops:
  7.2 49.9 %all-gather.6.cloned.1.call-start = ((), (), s32[]{:S(2)}) async-start(), calls=%async_computation.3 | async-start | bytes 6635520 | tf_op jit(solution)/shard_map/all_gather | solution.py:706
  10.4 96.2 %all-gather.8.cloned.1.call-start = ((), (), s32[]{:S(2)}) async-start(), calls=%async_computation.6 | async-start | bytes 6635520 | tf_op jit(solution)/shard_map/all_gather | solution.py:716
  19.9 215.6 %all-gather.10.cloned.1.call-start = ((), (), s32[]{:S(2)}) async-start(), calls=%async_computation.7 | async-start | bytes 28753920 | tf_op jit(solution)/shard_map/all_gather | solution.py:729
  67.6 524.3 %reduce-scatter.6.cloned.1.call-start = ((), (), s32[]{:S(2)}) async-start(), calls=%async_computation.4 | async-start | bytes 28753920 | tf_op jit(solution)/shard_map/reduce_scatter | solution.py:782
  126.5 25.3 %collective-permute-start.1 = (bf16[192,2560]{1,0:T(8,128)(2,1)}, bf16[192,2560]{1,0:T(8,128)(2,1)}, u32[]{:S(2)}, u32[]{:S(2)}) collective-permute-start(bf16[192,2560]{1,0:T(8,128)(2,1)} %get-tuple-element.173), channel_id=1, source_target_pairs={{0,1},{3,2},{4,5},{7,6},{8,9},{11,10},{12,13},{15,14},{16,17},{19,... | collective-permute-start | bytes 2949128 | tf_op jit(solution)/shard_map/ppermute | solution.py:612
  211.2 42.0 %collective-permute-start.7 = (bf16[192,2560]{1,0:T(8,128)(2,1)}, bf16[192,2560]{1,0:T(8,128)(2,1)}, u32[]{:S(2)}, u32[]{:S(2)}) collective-permute-start(bf16[192,2560]{1,0:T(8,128)(2,1)} %add_convert_fusion.22), channel_id=1, source_target_pairs={{1,2},{2,1},{5,6},{6,5},{9,10},{10,9},{13,14},{14,13},{17,18},{18,... | collective-permute-start | bytes 2949128 | tf_op jit(solution)/shard_map/ppermute | solution.py:616
  255.1 25.8 %collective-permute-start.9 = (bf16[192,2560]{1,0:T(8,128)(2,1)S(1)}, bf16[192,2560]{1,0:T(8,128)(2,1)S(1)}, u32[]{:S(2)}, u32[]{:S(2)}) collective-permute-start(bf16[192,2560]{1,0:T(8,128)(2,1)S(1)} %add_convert_fusion.19), channel_id=1, source_target_pairs={{1,0},{2,3},{5,4},{6,7},{9,8},{10,11},{13,12},{14,15},{17,16},{18,... | collective-permute-start | bytes 2949128 | tf_op jit(solution)/shard_map/ppermute | solution.py:609
  281.3 25.9 %collective-permute-start.10 = (bf16[192,2560]{1,0:T(8,128)(2,1)S(1)}, bf16[192,2560]{1,0:T(8,128)(2,1)S(1)}, u32[]{:S(2)}, u32[]{:S(2)}) collective-permute-start(bf16[192,2560]{1,0:T(8,128)(2,1)S(1)} %get-tuple-element.211), channel_id=1, source_target_pairs={{0,1},{3,2},{1,0},{2,3},{4,5},{7,6},{5,4},{6,7},{8,9},{11,10},{9,8... | collective-permute-start | bytes 2949128 | tf_op jit(solution)/shard_map/ppermute | solution.py:604
  307.4 24.7 %collective-permute-start.11 = (bf16[192,2560]{1,0:T(8,128)(2,1)S(1)}, bf16[192,2560]{1,0:T(8,128)(2,1)}, u32[]{:S(2)}, u32[]{:S(2)}) collective-permute-start(bf16[192,2560]{1,0:T(8,128)(2,1)S(1)} %get-tuple-element.221), channel_id=1, source_target_pairs={{0,1},{3,2},{4,5},{7,6},{8,9},{11,10},{12,13},{15,14},{16,17},{19,... | collective-permute-start | bytes 2949128 | tf_op jit(solution)/shard_map/ppermute | solution.py:612
  360.5 36.3 %collective-permute-start.15 = (bf16[192,2560]{1,0:T(8,128)(2,1)}, bf16[192,2560]{1,0:T(8,128)(2,1)}, u32[]{:S(2)}, u32[]{:S(2)}) collective-permute-start(bf16[192,2560]{1,0:T(8,128)(2,1)} %get-tuple-element.234), channel_id=1, source_target_pairs={{0,1},{3,2},{1,0},{2,3},{4,5},{7,6},{5,4},{6,7},{8,9},{11,10},{9,8... | collective-permute-start | bytes 2949128 | tf_op jit(solution)/shard_map/ppermute | solution.py:604
  399.5 250.1 %reduce-scatter.8.cloned.1.call-start = ((), (), s32[]{:S(2)}) async-start(), calls=%async_computation.5 | async-start | bytes 6635520 | tf_op jit(solution)/shard_map/reduce_scatter | solution.py:782
  403.1 24.8 %collective-permute-start.16 = (bf16[192,2560]{1,0:T(8,128)(2,1)S(1)}, bf16[192,2560]{1,0:T(8,128)(2,1)S(1)}, u32[]{:S(2)}, u32[]{:S(2)}) collective-permute-start(bf16[192,2560]{1,0:T(8,128)(2,1)S(1)} %copy-done.82), channel_id=1, source_target_pairs={{0,1},{3,2},{4,5},{7,6},{8,9},{11,10},{12,13},{15,14},{16,17},{19,... | collective-permute-start | bytes 2949128 | tf_op jit(solution)/shard_map/ppermute | solution.py:612
  479.3 112.6 %collective-permute-start.22 = (bf16[192,2560]{1,0:T(8,128)(2,1)}, bf16[192,2560]{1,0:T(8,128)(2,1)}, u32[]{:S(2)}, u32[]{:S(2)}) collective-permute-start(bf16[192,2560]{1,0:T(8,128)(2,1)} %get-tuple-element.268), channel_id=1, source_target_pairs={{0,1},{3,2},{1,0},{2,3},{4,5},{7,6},{5,4},{6,7},{8,9},{11,10},{9,8... | collective-permute-start | bytes 2949128 | tf_op jit(solution)/shard_map/ppermute | solution.py:604
  530.4 61.4 %collective-permute-start.23 = (bf16[192,2560]{1,0:T(8,128)(2,1)}, bf16[192,2560]{1,0:T(8,128)(2,1)}, u32[]{:S(2)}, u32[]{:S(2)}) collective-permute-start(bf16[192,2560]{1,0:T(8,128)(2,1)} %add_convert_fusion.8), channel_id=1, source_target_pairs={{1,2},{2,1},{5,6},{6,5},{9,10},{10,9},{13,14},{14,13},{17,18},{18,... | collective-permute-start | bytes 2949128 | tf_op jit(solution)/shard_map/ppermute | solution.py:616
  549.5 32.3 %collective-permute-start.26 = (bf16[264,768]{1,0:T(8,128)(2,1)}, bf16[264,768]{1,0:T(8,128)(2,1)}, u32[]{:S(2)}, u32[]{:S(2)}) collective-permute-start(bf16[264,768]{1,0:T(8,128)(2,1)} %get-tuple-element.283), channel_id=1, source_target_pairs={{0,1},{1,2},{2,3},{3,0},{4,5},{5,6},{6,7},{7,4},{8,9},{9,10},{10,1... | collective-permute-start | bytes 1216520 | tf_op jit(solution)/shard_map/ppermute | solution.py:639
  552.8 29.0 %collective-permute-start.25 = (bf16[264,768]{1,0:T(8,128)(2,1)}, bf16[264,768]{1,0:T(8,128)(2,1)}, u32[]{:S(2)}, u32[]{:S(2)}) collective-permute-start(bf16[264,768]{1,0:T(8,128)(2,1)} %get-tuple-element.282), channel_id=1, source_target_pairs={{0,2},{1,3},{2,0},{3,1},{4,6},{5,7},{6,4},{7,5},{8,10},{9,11},{10,... | collective-permute-start | bytes 1216520 | tf_op jit(solution)/shard_map/ppermute | solution.py:639
  552.8 29.0 %collective-permute-start.27 = (bf16[264,768]{1,0:T(8,128)(2,1)}, bf16[264,768]{1,0:T(8,128)(2,1)}, u32[]{:S(2)}, u32[]{:S(2)}) collective-permute-start(bf16[264,768]{1,0:T(8,128)(2,1)} %get-tuple-element.284), channel_id=1, source_target_pairs={{0,3},{1,0},{2,1},{3,2},{4,7},{5,4},{6,5},{7,6},{8,11},{9,8},{10,9... | collective-permute-start | bytes 1216520 | tf_op jit(solution)/shard_map/ppermute | solution.py:639
  583.2 33.3 %collective-permute-start.32 = (bf16[264,768]{1,0:T(8,128)(2,1)S(1)}, bf16[264,768]{1,0:T(8,128)(2,1)S(1)}, u32[]{:S(2)}, u32[]{:S(2)}) collective-permute-start(bf16[264,768]{1,0:T(8,128)(2,1)S(1)} %add_convert_fusion.27), channel_id=1, source_target_pairs={{3,0},{0,1},{1,2},{2,3},{7,4},{4,5},{5,6},{6,7},{11,8},{8,9},{9,10... | collective-permute-start | bytes 1216520 | tf_op jit(solution)/shard_map/ppermute | solution.py:648
  588.2 28.2 %collective-permute-start.31 = (bf16[264,768]{1,0:T(8,128)(2,1)S(1)}, bf16[264,768]{1,0:T(8,128)(2,1)S(1)}, u32[]{:S(2)}, u32[]{:S(2)}) collective-permute-start(bf16[264,768]{1,0:T(8,128)(2,1)S(1)} %add_convert_fusion.27), channel_id=1, source_target_pairs={{2,0},{3,1},{0,2},{1,3},{6,4},{7,5},{4,6},{5,7},{10,8},{11,9},{8,1... | collective-permute-start | bytes 1216520 | tf_op jit(solution)/shard_map/ppermute | solution.py:648
  591.9 131.8 %reduce-scatter.10.cloned.1.call-start = ((), (), s32[]{:S(2)}) async-start(), calls=%async_computation.8 | async-start | bytes 2211840
  598.0 43.9 %collective-permute-start.28 = (bf16[192,2560]{1,0:T(8,128)(2,1)}, bf16[192,2560]{1,0:T(8,128)(2,1)}, u32[]{:S(2)}, u32[]{:S(2)}) collective-permute-start(bf16[192,2560]{1,0:T(8,128)(2,1)} %get-tuple-element.297), channel_id=1, source_target_pairs={{0,1},{3,2},{1,0},{2,3},{4,5},{7,6},{5,4},{6,7},{8,9},{11,10},{9,8... | collective-permute-start | bytes 2949128 | tf_op jit(solution)/shard_map/ppermute | solution.py:604
  599.9 48.8 %collective-permute-start.29 = (bf16[192,2560]{1,0:T(8,128)(2,1)}, bf16[192,2560]{1,0:T(8,128)(2,1)}, u32[]{:S(2)}, u32[]{:S(2)}) collective-permute-start(bf16[192,2560]{1,0:T(8,128)(2,1)} %add_convert_fusion.6), channel_id=1, source_target_pairs={{1,2},{2,1},{5,6},{6,5},{9,10},{10,9},{13,14},{14,13},{17,18},{18,... | collective-permute-start | bytes 2949128 | tf_op jit(solution)/shard_map/ppermute | solution.py:616
  658.8 27.9 %collective-permute-start.33 = (bf16[192,2560]{1,0:T(8,128)(2,1)S(1)}, bf16[192,2560]{1,0:T(8,128)(2,1)}, u32[]{:S(2)}, u32[]{:S(2)}) collective-permute-start(bf16[192,2560]{1,0:T(8,128)(2,1)S(1)} %add_convert_fusion.3), channel_id=1, source_target_pairs={{1,0},{2,3},{5,4},{6,7},{9,8},{10,11},{13,12},{14,15},{17,16},{18,... | collective-permute-start | bytes 2949128 | tf_op jit(solution)/shard_map/ppermute | solution.py:609
  688.4 30.9 %collective-permute-start.35 = (bf16[192,2560]{1,0:T(8,128)(2,1)S(1)}, bf16[192,2560]{1,0:T(8,128)(2,1)S(1)}, u32[]{:S(2)}, u32[]{:S(2)}) collective-permute-start(bf16[192,2560]{1,0:T(8,128)(2,1)S(1)} %add_convert_fusion.2), channel_id=1, source_target_pairs={{1,0},{2,3},{5,4},{6,7},{9,8},{10,11},{13,12},{14,15},{17,16},{18,... | collective-permute-start | bytes 2949128 | tf_op jit(solution)/shard_map/ppermute | solution.py:609
  (149 other events, 1994.8 us)
Sparse Core Ops, SparseCore 0:
  10.5 46.5 all-gather.5
  59.6 46.9 all-gather.7
  108.5 126.9 all-gather.9
  399.6 166.7 reduce-scatter.5
  592.0 57.4 reduce-scatter.7
  669.5 50.0 reduce-scatter.9
where the time goes:
time: 749 us; the launch traced here: 735 us
  waiting for transfers between devices  247 us (33%)
  Pallas kernels  170 us (23%)
  other arithmetic  118 us (16%)
  starting transfers between devices  83.2 us (11%)
  local copies, waits for them, and re-layouts  61.1 us (8%)
  matrix products  38.5 us (5%)
  between operations  16.6 us (2%)
    ppermute x8, waiting for transfers between devices, step(): got = lax.ppermute(sends[0], 'tensor', inwards + outwards)  69.1 us
    ppermute x4, waiting for transfers between devices, step(): got = left = lax.ppermute(whole, 'tensor', outwards)  53.7 us
    dot_general x11, matrix products, contract(): lax.dot_general(left, right, (((left_dim,), (right_dim,)), ((), ())), pre...  38.5 us
    pallas_call x4, Pallas kernels, rows_product(): pl.pallas_call(kernel, out_shape=jax.ShapeDtypeStruct((tokens, width), bf...  38.1 us
    all_gather x1, waiting for transfers between devices, per_device(): lax.all_gather(jnp.concatenate([query_down, latent_down], axis=1), weight...  33.7 us
    pallas_call x2, Pallas kernels, ffn_front(): pl.pallas_call(kernel, out_shape=(given, given, given), grid=(pl.cdiv(uni...  32.7 us
    pallas_call x1, Pallas kernels, weight_grads(): pl.pallas_call(kernel, out_shape=jax.ShapeDtypeStruct((owners, count, row...  32.5 us
    unnamed x275, local copies, waits for them, and re-layouts  31.4 us
  transfers between devices with their start and end apart: 42, of which 18 were waited for; matrix products, arithmetic and copies ran while one was open for 23% of the time, Pallas kernels for 23%

commit v1 on v0

--- a/solution.py
+++ b/solution.py
@@ -587,35 +587,34 @@
             whole = low_sum_of(taken.pop(0), taken.pop(0))
         low = taken.pop(0) if fresh is not None else None
         joint = whole is not None and low is not None and whole.shape == low.shape
-        sends = [value for value in (half, whole) if value is not None]
         if joint:
-            sends.append(jnp.where(self.inner, whole, low))
-        elif low is not None:
-            sends.append(low)
+            whole, low = None, jnp.where(self.inner, whole, low)
+        sends = [value for value in (half, whole, low) if value is not None]
         if sends:
-            sends = lax.optimization_barrier(tuple(sends))
+            sends = list(lax.optimization_barrier(tuple(sends)))
             self.order.mark(sends[-1])
-        sends = list(sends)
         half = sends.pop(0) if half is not None else None
         whole = sends.pop(0) if whole is not None else None
+        low = sends.pop(0) if low is not None else None
         crossed, entered, left = None, None, None
         inwards, outwards = [(0, 1), (3, 2)], [(1, 0), (2, 3)]
         if joint:
-            got = lax.ppermute(sends[0], "tensor", inwards + outwards)
+            got = lax.ppermute(low, "tensor", inwards + outwards)
+            self.sums[self.crossed[0]] = (low, got)
+            entered = (fresh[0], fresh[1], got)
+        elif whole is not None:
+            got = left = lax.ppermute(whole, "tensor", outwards)
             self.sums[self.crossed[0]] = (whole, got)
-            entered = (fresh[0], sends[0], got)
-        else:
-            if whole is not None:
-                got = left = lax.ppermute(whole, "tensor", outwards)
-                self.sums[self.crossed[0]] = (whole, got)
-            if low is not None:
-                entered = (fresh[0], sends[0], lax.ppermute(sends[0], "tensor", inwards))
-        if joint:
-            entered = (fresh[0], low, got)
+        if low is not None and not joint:
+            entered = (fresh[0], low, lax.ppermute(low, "tensor", inwards))
         if half is not None:
             crossed = (self.entered[0], half, lax.ppermute(half, "tensor", [(1, 2), (2, 1)]))
         self.entered, self.crossed, self.left = entered, crossed, left
         return taken if len(taken) != 1 else taken[0]
+
+    def arrived(self):
+        got = [] if self.left is None else [self.left]
+        return got + [stage[2] for stage in (self.entered, self.crossed) if stage is not None]
 
     def done(self, keys):
         pieces = [jnp.where(self.inner, *self.sums[key]) for key in keys]
@@ -849,9 +848,7 @@
         [pack_grad[:, k * tokens : (k + 1) * tokens] for k in range(ctx_count)]
     )
     query_part = contract(query_up_all, jnp.concatenate(query_grads, axis=1), 1, 0)
-    low_part = jnp.concatenate([query_part, pack_local], axis=0).astype(bf16)
-    low_part = order.mark(held(order.take(low_part)))
-    low_finish = direct_sum(order, low_part)
+    query_part = order.mark(held(query_part.astype(bf16)))
     outs_grad = ups_grads(
         [order.take(part) for part in grad_attn],
         attended,
@@ -862,10 +859,12 @@
         owners,
     )
     order.mark(outs_grad)
+    pack_local = order.take(pack_local, order.last, *pipe.arrived())[0].astype(bf16)
+    low_part = order.mark(held(jnp.concatenate([query_part, pack_local], axis=0)))
+    low_finish = direct_sum(order, low_part)
+    outs_done = reduced(order.take(outs_grad))
     low_sums = low_finish()
-    outs_grad, ffn_done = order.take(outs_grad, ffn_done)
-    outs_done = reduced(outs_grad)
-    pipe.step()
+    ffn_done = pipe.step(ffn_done)
     both = order.take(low_sums).astype(f32)
     grad_query_latent, query_gain_grad = rms_back(
         both[:QRANK], query_latent, query_factor, query_gain
@@ -878,7 +877,7 @@
         axis=0,
     ).astype(bf16)
     lowered_grad = order.mark(held(lowered_grad))
-    outs_done = pipe.step(outs_done)
+    lowered_grad, outs_done = order.take(lowered_grad, outs_done)
     query_cols = QRANK // tensor_count
     latent_cols = (KVRANK + ROPE) // tensor_count
     cut = jnp.concatenate(
@@ -891,7 +890,8 @@
         axis=0,
     )
     down_cut = contract(norm_one, cut, 0, 1)
-    grad_norm_one = contract(lowered_grad, down_both, 0, 1)
+    grad_norm_one = order.mark(contract(lowered_grad, down_both, 0, 1))
+    pipe.step()
     _, first_gain_grad = rms_back(
         grad_norm_one, inputs.astype(f32), factor_one, first_gain, -1
     )

time: 749 us -> 746 us (level); the launches traced: 735 us -> 740 us
  starting transfers between devices: 83.2 us -> 122 us
  Pallas kernels: 170 us -> 159 us
  waiting for transfers between devices: 247 us -> 237 us
  other arithmetic: 118 us -> 110 us
    ppermute x1, starting transfers between devices: 6.56 us -> 30.4 us  [back_to_owners(): lax.ppermute(blocks[k], 'ctx', [(i, (i + k) % count) for i in range(count)])]
    ppermute x1, waiting for transfers between devices: 14.4 us -> 2.31 us  [back_to_owners(): lax.ppermute(blocks[k], 'ctx', [(i, (i + k) % count) for i in range(count)])]
    ppermute x3, starting transfers between devices: 7.84 us -> 17.5 us  [finish(): lax.ppermute(mine, 'tensor', [((i + k) % count, i) for i in range(count)])]
    unnamed x275 -> x259, local copies, waits for them, and re-layouts: 31.4 us -> 25.9 us
  transfers between devices with their start and end apart: 42 -> 42, of which waited for: 18 -> 18; matrix products, arithmetic and copies ran while one was open for 23% -> 23% of each run, Pallas kernels for 23% -> 21%
where the time goes in v1:
time: 746 us; the launch traced here: 740 us
  waiting for transfers between devices  237 us (32%)
  Pallas kernels  159 us (21%)
  starting transfers between devices  122 us (16%)
  other arithmetic  110 us (15%)
  local copies, waits for them, and re-layouts  57.1 us (8%)
  matrix products  38.6 us (5%)
  between operations  16.4 us (2%)
    ppermute x8, waiting for transfers between devices, step(): got = lax.ppermute(low, 'tensor', inwards + outwards)  64.9 us
    ppermute x4, waiting for transfers between devices, step(): got = left = lax.ppermute(whole, 'tensor', outwards)  49.4 us
    dot_general x11, matrix products, contract(): lax.dot_general(left, right, (((left_dim,), (right_dim,)), ((), ())), pre...  38.6 us
    pallas_call x4, Pallas kernels, rows_product(): pl.pallas_call(kernel, out_shape=jax.ShapeDtypeStruct((tokens, width), bf...  38.3 us
    all_gather x1, waiting for transfers between devices, per_device(): lax.all_gather(jnp.concatenate([query_down, latent_down], axis=1), weight...  33.7 us
    pallas_call x2, Pallas kernels, ffn_front(): pl.pallas_call(kernel, out_shape=(given, given, given), grid=(pl.cdiv(uni...  32.7 us
    pallas_call x1, Pallas kernels, weight_grads(): pl.pallas_call(kernel, out_shape=jax.ShapeDtypeStruct((owners, count, row...  32.5 us
    ppermute x8, starting transfers between devices, step(): got = lax.ppermute(low, 'tensor', inwards + outwards)  31.7 us
  transfers between devices with their start and end apart: 42, of which 18 were waited for; matrix products, arithmetic and copies ran while one was open for 23% of the time, Pallas kernels for 21%

profile of v1, /device:TPU:0, one launch (start us, length us, event | category | flops | bytes accessed | tf_op | source)
XLA Modules:
  0.0 740.1 jit_solution(3718019750861638859)
XLA Ops:
  23.5 33.7 %all-gather.6.cloned.1.call-done = bf16[2560,1056]{1,0:T(8,128)(2,1)} async-done(((bf16[320,1056]{1,0:T(8,128)(2,1)}), bf16[2560,1056]{1,0:T(8,128)(2,1)}) %all-gather.6.cloned.1.call-update) | async-done | bytes 5406736 | tf_op jit(solution)/shard_map/all_gather | solution.py:705
  57.1 10.5 %fusion.76 = f32[1056,768]{1,0:T(8,128)} fusion(bf16[2560,1056]{1,0:T(8,128)(2,1)} %all-gather.6.cloned.1.call-done, bf16[768,2560]{1,0:T(8,128)(2,1)} %fusion.4), kind=kOutput, calls=%fused_computation.220 | convolution fusion | flops 4152360960 | bytes 12582912 | tf_op jit(solution)/shard_map/dot_general | solution.py:29
  77.5 10.2 %collective-permute-done = bf16[288,768]{1,0:T(8,128)(2,1)S(1)} collective-permute-done((bf16[288,768]{1,0:T(8,128)(2,1)S(1)}, bf16[288,768]{1,0:T(8,128)(2,1)S(1)}, u32[]{:S(2)}, u32[]{:S(2)}) %collective-permute-start) | collective-permute-done | bytes 442400 | tf_op jit(solution)/shard_map/ppermute | solution.py:660
  90.1 16.5 %all-gather.8.cloned.1.call-done = bf16[4608,640]{1,0:T(8,128)(2,1)} async-done(((bf16[576,640]{1,0:T(8,128)(2,1)}), bf16[4608,640]{1,0:T(8,128)(2,1)}) %all-gather.8.cloned.1.call-update) | async-done | bytes 5898256 | tf_op jit(solution)/shard_map/all_gather | solution.py:715
  116.1 12.8 %attend.2 = (bf16[640,384]{1,0:T(8,128)(2,1)S(1)}, bf16[960,384]{1,0:T(8,128)(2,1)S(1)}, f32[10,1,384]{2,1,0:T(1,128)S(1)}) custom-call(s32[4]{0:T(128)S(1)} %dynamic_slice.24.refs_0_, f32[960,384]{1,0:T(8,128)S(1)} %get-tuple-element.323.refs_1_, f32[16,384]{1,0:T(8,128)S(1)} %get-tuple-element.351.refs_2_, f32[16,384]{1,0:T(8,128)S(1)} %get-tuple-element.344.refs_3_, ...), custom_call_target="tpu_custom_call" | custom-call | flops 3019898880 | bytes 3932160 | tf_op jit(solution)/shard_map/attend/pallas_call | solution.py:130
  146.2 11.1 %collective-permute-done.1 = bf16[192,2560]{1,0:T(8,128)(2,1)} collective-permute-done((bf16[192,2560]{1,0:T(8,128)(2,1)}, bf16[192,2560]{1,0:T(8,128)(2,1)}, u32[]{:S(2)}, u32[]{:S(2)}) %collective-permute-start.1) | collective-permute-done | bytes 983072 | tf_op jit(solution)/shard_map/ppermute | solution.py:609
  166.1 17.9 %collective-permute-done.2 = bf16[192,2560]{1,0:T(8,128)(2,1)S(1)} collective-permute-done((bf16[192,2560]{1,0:T(8,128)(2,1)S(1)}, bf16[192,2560]{1,0:T(8,128)(2,1)S(1)}, u32[]{:S(2)}, u32[]{:S(2)}) %collective-permute-start.2) | collective-permute-done | bytes 983072 | tf_op jit(solution)/shard_map/ppermute | solution.py:609
  192.8 19.6 %collective-permute-done.4 = bf16[192,2560]{1,0:T(8,128)(2,1)S(1)} collective-permute-done((bf16[192,2560]{1,0:T(8,128)(2,1)S(1)}, bf16[192,2560]{1,0:T(8,128)(2,1)S(1)}, u32[]{:S(2)}, u32[]{:S(2)}) %collective-permute-start.4) | collective-permute-done | bytes 983072 | tf_op jit(solution)/shard_map/ppermute | solution.py:602
  220.1 15.4 %collective-permute-done.6 = bf16[192,2560]{1,0:T(8,128)(2,1)S(1)} collective-permute-done((bf16[192,2560]{1,0:T(8,128)(2,1)S(1)}, bf16[192,2560]{1,0:T(8,128)(2,1)S(1)}, u32[]{:S(2)}, u32[]{:S(2)}) %collective-permute-start.6) | collective-permute-done | bytes 983072 | tf_op jit(solution)/shard_map/ppermute | solution.py:602
  240.5 16.0 %ffn_front.2 = (bf16[384,1600]{1,0:T(8,128)(2,1)S(1)}, bf16[384,1600]{1,0:T(8,128)(2,1)S(1)}, bf16[384,1600]{1,0:T(8,128)(2,1)S(1)}) custom-call(bf16[384,2560]{1,0:T(8,128)(2,1)S(1)} %multiply_convert_fusion.4.normed.refs_0_, bf16[384,2560]{1,0:T(8,128)(2,1)S(1)} %copy-done.8, bf16[8,3,320,1600]{3,2,1,0:T(8,128)(2,1)} %bitcast.107, ...), custom_call_target="tpu_custom_call" | custom-call | flops 9437184000 | bytes 24576000 | tf_op jit(solution)/shard_map/ffn_front/pallas_call | solution.py:311
  260.6 11.6 %rows_product.4 = bf16[384,2560]{1,0:T(8,128)(2,1)S(1)} custom-call(bf16[384,1600]{1,0:T(8,128)(2,1)S(1)} %get-tuple-element.195.refs_0_.refs_4_, bf16[384,1600]{1,0:T(8,128)(2,1)S(1)} %get-tuple-element.196.refs_1_.refs_6_, bf16[8,3,320,1600]{3,2,1,0:T(8,128)(2,1)} %bitcast.110, bf16[8,3,320,1600]{3,2,1,0:T(8,128)(2,1)} %bitcast.111), custom_call_target="tpu_custom_call" | custom-call | flops 6291456000 | bytes 16384000 | tf_op jit(solution)/shard_map/rows_product/pallas_call | solution.py:355
  293.1 11.5 %collective-permute-done.10 = bf16[192,2560]{1,0:T(8,128)(2,1)S(1)} collective-permute-done((bf16[192,2560]{1,0:T(8,128)(2,1)S(1)}, bf16[192,2560]{1,0:T(8,128)(2,1)S(1)}, u32[]{:S(2)}, u32[]{:S(2)}) %collective-permute-start.10) | collective-permute-done | bytes 983072 | tf_op jit(solution)/shard_map/ppermute | solution.py:602
  312.8 16.6 %ffn_front.3 = (bf16[384,1600]{1,0:T(8,128)(2,1)S(1)}, bf16[384,1600]{1,0:T(8,128)(2,1)S(1)}, bf16[384,1600]{1,0:T(8,128)(2,1)S(1)}) custom-call(bf16[384,2560]{1,0:T(8,128)(2,1)S(1)} %multiply_convert_fusion.3.normed.refs_1_, bf16[384,2560]{1,0:T(8,128)(2,1)S(1)} %copy-done.7, bf16[8,3,320,1600]{3,2,1,0:T(8,128)(2,1)} %bitcast.113, ...), custom_call_target="tpu_custom_call" | custom-call | flops 9437184000 | bytes 24576000 | tf_op jit(solution)/shard_map/ffn_front/pallas_call | solution.py:311
  333.7 11.6 %rows_product.6 = bf16[384,2560]{1,0:T(8,128)(2,1)S(1)} custom-call(bf16[384,1600]{1,0:T(8,128)(2,1)S(1)} %get-tuple-element.215.refs_0_.refs_5_, bf16[384,1600]{1,0:T(8,128)(2,1)S(1)} %get-tuple-element.216.refs_1_.refs_7_, bf16[8,3,320,1600]{3,2,1,0:T(8,128)(2,1)} %bitcast.116, bf16[8,3,320,1600]{3,2,1,0:T(8,128)(2,1)} %bitcast.117), custom_call_target="tpu_custom_call" | custom-call | flops 6291456000 | bytes 16384000 | tf_op jit(solution)/shard_map/rows_product/pallas_call | solution.py:355
  359.3 32.5 %weight_grads.1 = bf16[8,3,320,1600]{3,2,1,0:T(8,128)(2,1)} custom-call(bf16[384,2560]{1,0:T(8,128)(2,1)S(1)} %multiply_convert_fusion.4.normed.refs_0_, bf16[384,2560]{1,0:T(8,128)(2,1)} %copy-done.4, bf16[384,2560]{1,0:T(8,128)(2,1)} %get-tuple-element.221.grad.refs_2_, bf16[384,2560]{1,0:T(8,128)(2,1)} %get-tuple-element.222.grad.refs_3_, ...), custom_call_target="tpu_custom_call" | custom-call | flops 18874368000 | bytes 31948800 | tf_op jit(solution)/shard_map/weight_grads/pallas_call | solution.py:402
  413.1 14.9 %attend_back.2 = (bf16[960,384]{1,0:T(8,128)(2,1)S(1)}, bf16[1536,1280]{1,0:T(8,128)(2,1)S(1)}, f32[1536,128]{1,0:T(8,128)S(1)}) custom-call(s32[4]{0:T(128)S(1)} %dynamic_slice.24.refs_0_, bf16[960,384]{1,0:T(8,128)(2,1)S(1)} %get-tuple-element.228.refs_1_, f32[16,384]{1,0:T(8,128)S(1)} %copy-done.37, f32[16,384]{1,0:T(8,128)S(1)} %copy-done.35, ...), custom_call_target="tpu_custom_call" | custom-call | flops 7549747200 | bytes 7864320 | tf_op jit(solution)/shard_map/attend_back/pallas_call | solution.py:259
  463.7 14.2 %collective-permute-done.20 = bf16[192,2560]{1,0:T(8,128)(2,1)S(1)} collective-permute-done((bf16[192,2560]{1,0:T(8,128)(2,1)S(1)}, bf16[192,2560]{1,0:T(8,128)(2,1)S(1)}, u32[]{:S(2)}, u32[]{:S(2)}) %collective-permute-start.20) | collective-permute-done | bytes 983072 | tf_op jit(solution)/shard_map/ppermute | solution.py:602
  513.7 30.4 %collective-permute-start.24 = (bf16[288,768]{1,0:T(8,128)(2,1)}, bf16[288,768]{1,0:T(8,128)(2,1)}, u32[]{:S(2)}, u32[]{:S(2)}) collective-permute-start(bf16[288,768]{1,0:T(8,128)(2,1)} %pad_maximum_fusion.12), channel_id=1, source_target_pairs={{0,4},{4,0},{1,5},{5,1},{2,6},{6,2},{3,7},{7,3},{8,12},{12,8},{9,1... | collective-permute-start | bytes 1327112 | tf_op jit(solution)/shard_map/ppermute | solution.py:669
  547.7 10.5 %ups_grads.1 = bf16[8,576,640]{2,1,0:T(8,128)(2,1)} custom-call(bf16[384,2560]{1,0:T(8,128)(2,1)S(1)} %get-tuple-element.263.refs_0_, bf16[384,2560]{1,0:T(8,128)(2,1)S(1)} %copy-done.6, bf16[640,384]{1,0:T(8,128)(2,1)S(1)} %copy-done.23, bf16[640,384]{1,0:T(8,128)(2,1)S(1)} %copy-done.26, bf16[768,768]{1,0:T(8,128)(2,1)S(1)} %copy-done.12, ...), custom_call_target="tpu_custom_call" | custom-call | flops 4655677440 | bytes 9830400 | tf_op jit(solution)/shard_map/ups_grads/pallas_call | solution.py:489
  567.8 20.9 %collective-permute-done.25 = bf16[264,768]{1,0:T(8,128)(2,1)S(1)} collective-permute-done((bf16[264,768]{1,0:T(8,128)(2,1)S(1)}, bf16[264,768]{1,0:T(8,128)(2,1)S(1)}, u32[]{:S(2)}, u32[]{:S(2)}) %collective-permute-start.25) | collective-permute-done | bytes 405536 | tf_op jit(solution)/shard_map/ppermute | solution.py:638
  588.9 15.1 %collective-permute-start.32 = (bf16[264,768]{1,0:T(8,128)(2,1)S(1)}, bf16[264,768]{1,0:T(8,128)(2,1)S(1)}, u32[]{:S(2)}, u32[]{:S(2)}) collective-permute-start(bf16[264,768]{1,0:T(8,128)(2,1)S(1)} %add_convert_fusion.26), channel_id=1, source_target_pairs={{3,0},{0,1},{1,2},{2,3},{7,4},{4,5},{5,6},{6,7},{11,8},{8,9},{9,10... | collective-permute-start | bytes 1216520 | tf_op jit(solution)/shard_map/ppermute | solution.py:647
  642.0 10.8 %fusion.5 = (bf16[2560]{0:T(1024)(128)(2,1)S(1)}, f32[768,2560]{1,0:T(8,128)}) fusion(bf16[1,768,2560]{2,1,0:T(8,128)(2,1)} %param.15, f32[768]{0:T(1024)S(1)} %copy-done.104, bf16[1056,768]{1,0:T(8,128)(2,1)} %pad_maximum_fusion.6, bf16[2560,1056]{1,0:T(8,128)(2,1)} %all-gather.6.cloned.1.call-done), kind=kOutput, calls=%fused_computation.7 | convolution fusion | flops 4160222720 | bytes 18833408 | tf_op jit(solution)/shard_map/dot_general | solution.py:29
  675.4 11.0 %fusion.10 = f32[1,768,2560]{2,1,0:T(8,128)} fusion(f32[384,2560]{1,0:T(8,128)} %get-tuple-element.307, f32[384,2560]{1,0:T(8,128)} %get-tuple-element.309, f32[768,2560]{1,0:T(8,128)} %get-tuple-element.293, bf16[1,768,2560]{2,1,0:T(8,128)(2,1)} %param.15, f32[768]{0:T(1024)S(1)} %broadcast_multiply_fusion.2, f32[2560]{0:T(1024)S(1)} %copy-done.101, ...), kind=kLoop, calls=%fused_computation.12 | loop fusion | flops 15728640 | bytes 27541504 | tf_op jit(solution)/shard_map/broadcast_in_dim | solution.py:928
  693.8 30.7 %collective-permute-done.35 = bf16[192,2560]{1,0:T(8,128)(2,1)S(1)} collective-permute-done((bf16[192,2560]{1,0:T(8,128)(2,1)S(1)}, bf16[192,2560]{1,0:T(8,128)(2,1)S(1)}, u32[]{:S(2)}, u32[]{:S(2)}) %collective-permute-start.35) | collective-permute-done | bytes 983072 | tf_op jit(solution)/shard_map/ppermute | solution.py:606
  (491 shorter events, 317.9 us)
Async XLA Ops:
  7.2 49.9 %all-gather.6.cloned.1.call-start = ((), (), s32[]{:S(2)}) async-start(), calls=%async_computation.3 | async-start | bytes 6635520 | tf_op jit(solution)/shard_map/all_gather | solution.py:705
  10.4 96.2 %all-gather.8.cloned.1.call-start = ((), (), s32[]{:S(2)}) async-start(), calls=%async_computation.6 | async-start | bytes 6635520 | tf_op jit(solution)/shard_map/all_gather | solution.py:715
  20.0 219.0 %all-gather.10.cloned.1.call-start = ((), (), s32[]{:S(2)}) async-start(), calls=%async_computation.7 | async-start | bytes 28753920 | tf_op jit(solution)/shard_map/all_gather | solution.py:728
  67.6 553.0 %reduce-scatter.6.cloned.1.call-start = ((), (), s32[]{:S(2)}) async-start(), calls=%async_computation.4 | async-start | bytes 28753920 | tf_op jit(solution)/shard_map/reduce_scatter | solution.py:781
  132.1 25.1 %collective-permute-start.1 = (bf16[192,2560]{1,0:T(8,128)(2,1)}, bf16[192,2560]{1,0:T(8,128)(2,1)}, u32[]{:S(2)}, u32[]{:S(2)}) collective-permute-start(bf16[192,2560]{1,0:T(8,128)(2,1)} %get-tuple-element.164), channel_id=1, source_target_pairs={{0,1},{3,2},{4,5},{7,6},{8,9},{11,10},{12,13},{15,14},{16,17},{19,... | collective-permute-start | bytes 2949128 | tf_op jit(solution)/shard_map/ppermute | solution.py:609
  159.0 25.0 %collective-permute-start.2 = (bf16[192,2560]{1,0:T(8,128)(2,1)S(1)}, bf16[192,2560]{1,0:T(8,128)(2,1)S(1)}, u32[]{:S(2)}, u32[]{:S(2)}) collective-permute-start(bf16[192,2560]{1,0:T(8,128)(2,1)S(1)} %copy-done.78), channel_id=1, source_target_pairs={{0,1},{3,2},{4,5},{7,6},{8,9},{11,10},{12,13},{15,14},{16,17},{19,... | collective-permute-start | bytes 2949128 | tf_op jit(solution)/shard_map/ppermute | solution.py:609
  185.5 26.8 %collective-permute-start.4 = (bf16[192,2560]{1,0:T(8,128)(2,1)S(1)}, bf16[192,2560]{1,0:T(8,128)(2,1)S(1)}, u32[]{:S(2)}, u32[]{:S(2)}) collective-permute-start(bf16[192,2560]{1,0:T(8,128)(2,1)S(1)} %fusion.27), channel_id=1, source_target_pairs={{0,1},{3,2},{1,0},{2,3},{4,5},{7,6},{5,4},{6,7},{8,9},{11,10},{9,8... | collective-permute-start | bytes 2949128 | tf_op jit(solution)/shard_map/ppermute | solution.py:602
  217.9 38.6 %collective-permute-start.7 = (bf16[192,2560]{1,0:T(8,128)(2,1)}, bf16[192,2560]{1,0:T(8,128)(2,1)}, u32[]{:S(2)}, u32[]{:S(2)}) collective-permute-start(bf16[192,2560]{1,0:T(8,128)(2,1)} %add_convert_fusion.22), channel_id=1, source_target_pairs={{1,2},{2,1},{5,6},{6,5},{9,10},{10,9},{13,14},{14,13},{17,18},{18,... | collective-permute-start | bytes 2949128 | tf_op jit(solution)/shard_map/ppermute | solution.py:611
  281.5 23.1 %collective-permute-start.10 = (bf16[192,2560]{1,0:T(8,128)(2,1)S(1)}, bf16[192,2560]{1,0:T(8,128)(2,1)S(1)}, u32[]{:S(2)}, u32[]{:S(2)}) collective-permute-start(bf16[192,2560]{1,0:T(8,128)(2,1)S(1)} %fusion.29), channel_id=1, source_target_pairs={{0,1},{3,2},{1,0},{2,3},{4,5},{7,6},{5,4},{6,7},{8,9},{11,10},{9,8... | collective-permute-start | bytes 2949128 | tf_op jit(solution)/shard_map/ppermute | solution.py:602
  304.8 24.7 %collective-permute-start.11 = (bf16[192,2560]{1,0:T(8,128)(2,1)S(1)}, bf16[192,2560]{1,0:T(8,128)(2,1)}, u32[]{:S(2)}, u32[]{:S(2)}) collective-permute-start(bf16[192,2560]{1,0:T(8,128)(2,1)S(1)} %get-tuple-element.210), channel_id=1, source_target_pairs={{0,1},{3,2},{4,5},{7,6},{8,9},{11,10},{12,13},{15,14},{16,17},{19,... | collective-permute-start | bytes 2949128 | tf_op jit(solution)/shard_map/ppermute | solution.py:609
  354.8 37.1 %collective-permute-start.15 = (bf16[192,2560]{1,0:T(8,128)(2,1)}, bf16[192,2560]{1,0:T(8,128)(2,1)}, u32[]{:S(2)}, u32[]{:S(2)}) collective-permute-start(bf16[192,2560]{1,0:T(8,128)(2,1)} %fusion.30), channel_id=1, source_target_pairs={{0,1},{3,2},{1,0},{2,3},{4,5},{7,6},{5,4},{6,7},{8,9},{11,10},{9,8... | collective-permute-start | bytes 2949128 | tf_op jit(solution)/shard_map/ppermute | solution.py:602
  394.6 240.3 %reduce-scatter.8.cloned.1.call-start = ((), (), s32[]{:S(2)}) async-start(), calls=%async_computation.5 | async-start | bytes 6635520 | tf_op jit(solution)/shard_map/reduce_scatter | solution.py:781
  398.2 29.8 %collective-permute-start.16 = (bf16[192,2560]{1,0:T(8,128)(2,1)S(1)}, bf16[192,2560]{1,0:T(8,128)(2,1)S(1)}, u32[]{:S(2)}, u32[]{:S(2)}) collective-permute-start(bf16[192,2560]{1,0:T(8,128)(2,1)S(1)} %copy-done.76), channel_id=1, source_target_pairs={{0,1},{3,2},{4,5},{7,6},{8,9},{11,10},{12,13},{15,14},{16,17},{19,... | collective-permute-start | bytes 2949128 | tf_op jit(solution)/shard_map/ppermute | solution.py:609
  402.5 25.6 %collective-permute-start.17 = (bf16[192,2560]{1,0:T(8,128)(2,1)S(1)}, bf16[192,2560]{1,0:T(8,128)(2,1)S(1)}, u32[]{:S(2)}, u32[]{:S(2)}) collective-permute-start(bf16[192,2560]{1,0:T(8,128)(2,1)S(1)} %copy-done.77), channel_id=1, source_target_pairs={{1,2},{2,1},{5,6},{6,5},{9,10},{10,9},{13,14},{14,13},{17,18},{18,... | collective-permute-start | bytes 2949128 | tf_op jit(solution)/shard_map/ppermute | solution.py:611
  480.5 81.2 %collective-permute-start.22 = (bf16[192,2560]{1,0:T(8,128)(2,1)}, bf16[192,2560]{1,0:T(8,128)(2,1)}, u32[]{:S(2)}, u32[]{:S(2)}) collective-permute-start(bf16[192,2560]{1,0:T(8,128)(2,1)} %fusion.33), channel_id=1, source_target_pairs={{0,1},{3,2},{1,0},{2,3},{4,5},{7,6},{5,4},{6,7},{8,9},{11,10},{9,8... | collective-permute-start | bytes 2949128 | tf_op jit(solution)/shard_map/ppermute | solution.py:602
  482.6 79.0 %collective-permute-start.23 = (bf16[192,2560]{1,0:T(8,128)(2,1)}, bf16[192,2560]{1,0:T(8,128)(2,1)}, u32[]{:S(2)}, u32[]{:S(2)}) collective-permute-start(bf16[192,2560]{1,0:T(8,128)(2,1)} %add_convert_fusion.8), channel_id=1, source_target_pairs={{1,2},{2,1},{5,6},{6,5},{9,10},{10,9},{13,14},{14,13},{17,18},{18,... | collective-permute-start | bytes 2949128 | tf_op jit(solution)/shard_map/ppermute | solution.py:611
  513.7 46.8 %collective-permute-start.24 = (bf16[288,768]{1,0:T(8,128)(2,1)}, bf16[288,768]{1,0:T(8,128)(2,1)}, u32[]{:S(2)}, u32[]{:S(2)}) collective-permute-start(bf16[288,768]{1,0:T(8,128)(2,1)} %pad_maximum_fusion.12), channel_id=1, source_target_pairs={{0,4},{4,0},{1,5},{5,1},{2,6},{6,2},{3,7},{7,3},{8,12},{12,8},{9,1... | collective-permute-start | bytes 1327112 | tf_op jit(solution)/shard_map/ppermute | solution.py:669
  563.3 165.5 %reduce-scatter.10.cloned.1.call-start = ((), (), s32[]{:S(2)}) async-start(), calls=%async_computation.8 | async-start | bytes 2211840
  563.3 25.4 %collective-permute-start.25 = (bf16[264,768]{1,0:T(8,128)(2,1)S(1)}, bf16[264,768]{1,0:T(8,128)(2,1)S(1)}, u32[]{:S(2)}, u32[]{:S(2)}) collective-permute-start(bf16[264,768]{1,0:T(8,128)(2,1)S(1)} %get-tuple-element.267), channel_id=1, source_target_pairs={{0,2},{1,3},{2,0},{3,1},{4,6},{5,7},{6,4},{7,5},{8,10},{9,11},{10,... | collective-permute-start | bytes 1216520 | tf_op jit(solution)/shard_map/ppermute | solution.py:638
  565.5 23.2 %collective-permute-start.27 = (bf16[264,768]{1,0:T(8,128)(2,1)S(1)}, bf16[264,768]{1,0:T(8,128)(2,1)S(1)}, u32[]{:S(2)}, u32[]{:S(2)}) collective-permute-start(bf16[264,768]{1,0:T(8,128)(2,1)S(1)} %get-tuple-element.269), channel_id=1, source_target_pairs={{0,3},{1,0},{2,1},{3,2},{4,7},{5,4},{6,5},{7,6},{8,11},{9,8},{10,9... | collective-permute-start | bytes 1216520 | tf_op jit(solution)/shard_map/ppermute | solution.py:638
  588.9 30.2 %collective-permute-start.32 = (bf16[264,768]{1,0:T(8,128)(2,1)S(1)}, bf16[264,768]{1,0:T(8,128)(2,1)S(1)}, u32[]{:S(2)}, u32[]{:S(2)}) collective-permute-start(bf16[264,768]{1,0:T(8,128)(2,1)S(1)} %add_convert_fusion.26), channel_id=1, source_target_pairs={{3,0},{0,1},{1,2},{2,3},{7,4},{4,5},{5,6},{6,7},{11,8},{8,9},{9,10... | collective-permute-start | bytes 1216520 | tf_op jit(solution)/shard_map/ppermute | solution.py:647
  626.0 35.1 %collective-permute-start.28 = (bf16[192,2560]{1,0:T(8,128)(2,1)}, bf16[192,2560]{1,0:T(8,128)(2,1)S(1)}, u32[]{:S(2)}, u32[]{:S(2)}) collective-permute-start(bf16[192,2560]{1,0:T(8,128)(2,1)} %fusion.34), channel_id=1, source_target_pairs={{0,1},{3,2},{1,0},{2,3},{4,5},{7,6},{5,4},{6,7},{8,9},{11,10},{9,8... | collective-permute-start | bytes 2949128 | tf_op jit(solution)/shard_map/ppermute | solution.py:602
  664.0 25.4 %collective-permute-start.33 = (bf16[192,2560]{1,0:T(8,128)(2,1)S(1)}, bf16[192,2560]{1,0:T(8,128)(2,1)}, u32[]{:S(2)}, u32[]{:S(2)}) collective-permute-start(bf16[192,2560]{1,0:T(8,128)(2,1)S(1)} %add_convert_fusion.3), channel_id=1, source_target_pairs={{1,0},{2,3},{5,4},{6,7},{9,8},{10,11},{13,12},{14,15},{17,16},{18,... | collective-permute-start | bytes 2949128 | tf_op jit(solution)/shard_map/ppermute | solution.py:606
  690.8 33.7 %collective-permute-start.35 = (bf16[192,2560]{1,0:T(8,128)(2,1)S(1)}, bf16[192,2560]{1,0:T(8,128)(2,1)S(1)}, u32[]{:S(2)}, u32[]{:S(2)}) collective-permute-start(bf16[192,2560]{1,0:T(8,128)(2,1)S(1)} %add_convert_fusion.2), channel_id=1, source_target_pairs={{1,0},{2,3},{5,4},{6,7},{9,8},{10,11},{13,12},{14,15},{17,16},{18,... | collective-permute-start | bytes 2949128 | tf_op jit(solution)/shard_map/ppermute | solution.py:606
  (141 other events, 1955.6 us)
Sparse Core Ops, SparseCore 0:
  10.5 46.5 all-gather.5
  59.6 46.9 all-gather.7
  108.5 126.9 all-gather.9
  394.7 175.3 reduce-scatter.5
  574.4 59.6 reduce-scatter.7
  675.5 48.3 reduce-scatter.9
